TPU v7x, 32 devices: a whole 2x2x4 slice. The times are simulated.
32 devices in a mesh: grp: 2 (over y), wide: 16 (over z, x, core).
Axes of the slice: x: 2, y: 2, z: 4, core: 2. Of those that a mesh axis runs over, the one named last changes fastest.
Arguments:
- coeff: float32 [256, 6144], P(('grp', 'wide')), may hold values from -6 to 6
- beta_blocks: float32 [96, 128, 128], replicated, may hold values from -0.5 to 0.5
- block_list: int32 [2, 96], replicated, may hold values from 0 to 47
- alpha_blocks: float32 [32, 2, 8, 8], P(('grp', 'wide')), may hold values from -2 to 2
- partner_mask: int32 [32, 2], P(('grp', 'wide')), may hold values 0 or 1
- exc_source: int32 [90, 256], P(None, 'grp'), may hold values from 0 to 255
- exc_pair: int32 [90, 256], P(None, 'grp'), may hold values from 0 to 323
- exc_parity: int32 [90, 256], P(None, 'grp'), may hold values from 0 to 1
- occupation: int32 [18, 6144], P(None, 'wide'), may hold values 0 or 1
- coulomb: float32 [324, 18], replicated, may hold values from -0.2 to 0.2
Outputs:
- sigma: float32 [256, 6144], P(('grp', 'wide'))
Inputs may be any that keep to these rules, and one draw needn't show every extreme that they name: `exc_source`: any alpha string.
All inputs are finite; a program needn't handle non-finite values. No bound on the sum of `partner_mask` or of `occupation` on one device may be relied on, other than what follows from the above.
Results may differ from a plain program's by a relative error of at most 0.0003.
Values sent between devices are 32-bit elements; how exact they have to be, the bound alone decides.
A program may use at most 128 MiB of HBM per device.

v0:
```python
import jax
import jax.numpy as jnp
from jax import lax
from jax.sharding import PartitionSpec as P

HIGH = lax.Precision.HIGHEST


def per_device(
    coeff,
    beta_blocks,
    block_list,
    alpha_blocks,
    partner_mask,
    exc_source,
    exc_pair,
    exc_parity,
    occupation,
    coulomb,
):
    alpha_rows, beta_width = coeff.shape
    block_size = beta_blocks.shape[1]
    block_count = beta_width // block_size
    blocked = coeff.reshape(alpha_rows, block_count, block_size)
    block_ids = jnp.arange(block_count, dtype=jnp.int32)
    choosing = (block_list[0][:, None] == block_ids[None, :]).astype(jnp.float32)
    picked = jnp.einsum("rnk,pn->rpk", blocked, choosing, precision=HIGH)
    applied = jnp.einsum("rpk,pkl->rpl", picked, beta_blocks, precision=HIGH)
    placing = (block_list[1][:, None] == block_ids[None, :]).astype(jnp.float32)
    same_beta = jnp.einsum("rpl,pn->rnl", applied, placing, precision=HIGH).reshape(
        alpha_rows, beta_width
    )
    masked = alpha_blocks[0] * partner_mask[0][:, None, None].astype(jnp.float32)
    group_count = masked.shape[0]
    coupling = masked.transpose(1, 0, 2).reshape(alpha_rows, group_count * alpha_rows)
    same_alpha = jnp.dot(
        coupling,
        lax.all_gather(coeff, "grp", axis=0, tiled=True),
        precision=HIGH,
        preferred_element_type=jnp.float32,
    )
    beta_major = lax.all_to_all(coeff, "wide", split_axis=1, concat_axis=0, tiled=True)
    every_string = lax.all_gather(beta_major, "grp", axis=0, tiled=True)
    group_rows, slice_width = beta_major.shape
    replace_count = exc_source.shape[0]
    weights_local = jnp.dot(
        coulomb, occupation.astype(jnp.float32), precision=HIGH, preferred_element_type=jnp.float32
    )
    phases = 1.0 - 2.0 * exc_parity.astype(jnp.float32)
    row_block = 256 if group_rows % 256 == 0 else group_rows
    turns = group_rows // row_block

    def one_block(entry):
        sources, pairs, signs = entry
        fetched = jnp.take(every_string, sources, axis=0)
        factor = jnp.take(weights_local, pairs, axis=0)
        return jnp.sum(signs[:, :, None] * factor * fetched, axis=1)

    mixed_local = lax.map(
        one_block,
        (
            exc_source.T.reshape(turns, row_block, replace_count),
            exc_pair.T.reshape(turns, row_block, replace_count),
            phases.T.reshape(turns, row_block, replace_count),
        ),
    ).reshape(group_rows, slice_width)
    mixed = lax.all_to_all(mixed_local, "wide", split_axis=0, concat_axis=1, tiled=True)
    return same_beta + same_alpha + mixed


def solution(mesh):
    in_specs = (
        P(("grp", "wide"), None),
        P(),
        P(),
        P(("grp", "wide"), None, None, None),
        P(("grp", "wide"), None),
        P(None, "grp"),
        P(None, "grp"),
        P(None, "grp"),
        P(None, "wide"),
        P(),
    )
    out_specs = P(("grp", "wide"), None)
    return jax.shard_map(
        per_device, mesh=mesh, in_specs=in_specs, out_specs=out_specs, check_vma=False
    )
```

profile of v0, /device:TPU:0, one launch (start us, length us, event | category | flops | bytes accessed | tf_op | source)
XLA Modules:
  0.0 152.9 jit_solution(176916170350364619)
XLA Ops:
  0.0 7.5 %all-to-all-start = ((f32[8,16,384]{2,0,1:T(8,128)}), f32[8,16,384]{2,0,1:T(8,128)S(1)}, u32[]{:S(2)}, u32[]{:S(2)}) async-start(f32[8,16,384]{2,0,1:T(8,128)} %bitcast.52), calls=%async_computation | async-start | bytes 393216 | tf_op jit(solution)/shard_map/all_to_all | solution.py:42
  7.5 0.8 compare_select_fusion
  8.3 0.8 compare_and_fusion
  9.1 0.8 compare_select_fusion.1
  9.9 0.8 compare_and_fusion.1
  10.8 0.1 copy.20
  10.9 0.1 reshape.61
  11.1 0.1 reshape.53
  11.3 1.5 fusion.10
  12.8 29.0 %gather_fusion = f32[11520,384]{1,0:T(8,128)} fusion(f32[324,384]{1,0:T(8,128)S(1)} %fusion.10, s32[12288]{0:T(1024)S(1)} %pad_clamp_fusion.1), kind=kCustom, calls=%fused_computation | custom fusion | bytes 35435520 | tf_op jit(solution)/shard_map/while/body/eval_jaxpr/jit(_take)/gather | solution.py:56
  41.9 18.5 %reshape.52 = f32[128,90,384]{2,1,0:T(8,128)} reshape(f32[11520,384]{1,0:T(8,128)} %gather_fusion) | data formatting | bytes 35389440 | tf_op jit(solution)/shard_map/while/body/eval_jaxpr/jit(_take)/gather | solution.py:56
  60.5 0.1 copy.19
  60.6 0.1 copy.17
  60.8 0.3 fusion.6
  61.2 7.5 %fusion.2 = f32[96,8,128]{2,1,0:T(8,128)S(1)} fusion(f32[96,128,128]{2,1,0:T(8,128)} %param.11, f32[96,8,128]{2,0,1:T(8,128)S(1)} %fusion.6), kind=kOutput, calls=%fused_computation.7 | convolution fusion | flops 150994944 | bytes 7077888 | tf_op jit(solution)/shard_map/rpk,pkl->rpl/dot_general | solution.py:28
  68.6 7.9 %all_gather.7 = f32[256,384]{1,0:T(8,128)S(1)} all-gather(f32[128,384]{1,0:T(8,128)S(1)} %bitcast.54), channel_id=1, replica_groups=mesh['grp'=2,'wide'=16] {'grp'}, dimensions={0}, use_global_device_ids=true | all-gather | bytes 589824 | tf_op jit(solution)/shard_map/all_gather | solution.py:43
  76.6 29.0 %gather_fusion.1 = f32[11520,384]{1,0:T(8,128)} fusion(f32[256,384]{1,0:T(8,128)S(1)} %all_gather.7, s32[12288]{0:T(1024)S(1)} %pad_clamp_fusion), kind=kCustom, calls=%fused_computation.1 | custom fusion | bytes 35435520 | tf_op jit(solution)/shard_map/while/body/eval_jaxpr/jit(_take)/gather | solution.py:55
  105.6 18.5 %reshape.60 = f32[128,90,384]{2,1,0:T(8,128)} reshape(f32[11520,384]{1,0:T(8,128)} %gather_fusion.1) | data formatting | bytes 35389440 | tf_op jit(solution)/shard_map/while/body/eval_jaxpr/jit(_take)/gather | solution.py:55
  124.1 13.1 %multiply_reduce_fusion = f32[128,384]{1,0:T(8,128)} fusion(f32[128,90,384]{2,1,0:T(8,128)} %reshape.60, f32[128,90,384]{2,1,0:T(8,128)} %reshape.52, f32[128,90]{1,0:T(8,128)S(1)} %copy.16, pred[128,90]{1,0:T(8,128)(4,1)S(1)} %copy.19, pred[128,90]{1,0:T(8,128)(4,1)S(1)} %copy.17), kind=kLoop, calls=%fused_computation.2 | loop fusion | flops 22069248 | bytes 35655168 | tf_op jit(solution)/shard_map/while/body/eval_jaxpr/reduce_sum | solution.py:57
  137.2 5.7 %all-to-all-start.1 = ((f32[16,8,384]{2,1,0:T(8,128)}), f32[16,8,384]{2,1,0:T(8,128)S(1)}, u32[]{:S(2)}, u32[]{:S(2)}) async-start(f32[16,8,384]{2,1,0:T(8,128)} %bitcast.17), calls=%async_computation.1 | async-start | bytes 393216 | tf_op jit(solution)/shard_map/all_to_all | solution.py:67
  143.1 7.9 %all_gather.6 = f32[16,6144]{1,0:T(8,128)S(1)} all-gather(f32[8,6144]{1,0:T(8,128)S(1)} %copy-done.2), channel_id=1, replica_groups=mesh['grp'=2,'wide'=16] {'grp'}, dimensions={0}, use_global_device_ids=true | all-gather | bytes 589824 | tf_op jit(solution)/shard_map/all_gather | solution.py:38
  151.0 0.3 convolution_bitcast_fusion
  151.3 0.6 all-to-all-done.1
  151.9 1.0 fusion
  (25 shorter events, 0.4 us)
Async XLA Ops:
  0.0 11.3 %copy-start = (f32[324,18]{0,1:T(8,128)S(1)}, f32[324,18]{0,1:T(8,128)}, u32[]{:S(2)}) copy-start(f32[324,18]{0,1:T(8,128)} %param.19) | copy-start | bytes 69988
  0.0 68.6 %all-to-all-start = ((f32[8,16,384]{2,0,1:T(8,128)}), f32[8,16,384]{2,0,1:T(8,128)S(1)}, u32[]{:S(2)}, u32[]{:S(2)}) async-start(f32[8,16,384]{2,0,1:T(8,128)} %bitcast.52), calls=%async_computation | async-start | bytes 393216 | tf_op jit(solution)/shard_map/all_to_all | solution.py:42
  41.8 18.6 %copy-start.3 = (s32[90,128]{1,0:T(8,128)S(1)}, s32[90,128]{1,0:T(8,128)}, u32[]{:S(2)}) copy-start(s32[90,128]{1,0:T(8,128)} %param.17) | copy-start | bytes 138244
  41.9 18.9 %copy-start.6 = (s32[1,2]{1,0:T(1,128)S(1)}, s32[1,2]{1,0:T(1,128)}, u32[]{:S(2)}) copy-start(s32[1,2]{1,0:T(1,128)} %param.14) | copy-start | bytes 28
  41.9 18.9 %copy-start.5 = (s32[2,96]{1,0:T(2,128)S(1)}, s32[2,96]{1,0:T(2,128)}, u32[]{:S(2)}) copy-start(s32[2,96]{1,0:T(2,128)} %param.12) | copy-start | bytes 2308
  41.9 19.0 %copy-start.2 = (f32[8,6144]{1,0:T(8,128)S(1)}, f32[8,6144]{1,0:T(8,128)}, u32[]{:S(2)}) copy-start(f32[8,6144]{1,0:T(8,128)} %param.10) | copy-start | bytes 589828
  105.6 47.3 %copy-start.1 = (f32[324,18]{0,1:T(8,128)S(1)}, f32[324,18]{0,1:T(8,128)}, u32[]{:S(2)}) copy-start(f32[324,18]{0,1:T(8,128)} %param.19) | copy-start | bytes 69988
  124.1 18.8 %copy-start.4 = (f32[1,2,8,8]{3,2,1,0:T(8,128)S(1)}, f32[1,2,8,8]{3,2,1,0:T(8,128)}, u32[]{:S(2)}) copy-start(f32[1,2,8,8]{3,2,1,0:T(8,128)} %param.13) | copy-start | bytes 1540
  137.2 14.7 %all-to-all-start.1 = ((f32[16,8,384]{2,1,0:T(8,128)}), f32[16,8,384]{2,1,0:T(8,128)S(1)}, u32[]{:S(2)}, u32[]{:S(2)}) async-start(f32[16,8,384]{2,1,0:T(8,128)} %bitcast.17), calls=%async_computation.1 | async-start | bytes 393216 | tf_op jit(solution)/shard_map/all_to_all | solution.py:67
where the time goes:
time: 154 us; the launch traced here: 153 us
  local copies, waits for them, and re-layouts  96.1 us (62%)
  other arithmetic  16.4 us (11%)
  blocking collectives  15.8 us (10%)
  starting transfers between devices  13.2 us (9%)
  matrix products  10.6 us (7%)
    gather x2, local copies, waits for them, and re-layouts, one_block(): factor = jnp.take(weights_local, pairs, axis=0)  47.6 us
    gather x2, local copies, waits for them, and re-layouts, one_block(): fetched = jnp.take(every_string, sources, axis=0)  47.5 us
    reduce_sum x1, other arithmetic, one_block(): return jnp.sum(signs[:, :, None] * factor * fetched, axis=1)  13.1 us
    all_gather x1, blocking collectives, per_device(): every_string = lax.all_gather(beta_major, 'grp', axis=0, tiled=True)  7.91 us
    all_gather x1, blocking collectives, per_device(): lax.all_gather(coeff, 'grp', axis=0, tiled=True)  7.91 us
    all_to_all x1, starting transfers between devices, per_device(): lax.all_to_all(coeff, 'wide', split_axis=1, concat_axis=0, tiled=True)  7.49 us
    dot_general x1, matrix products, per_device(): applied = jnp.einsum('rpk,pkl->rpl', picked, beta_blocks, precision=HIGH)  7.45 us
    all_to_all x1, starting transfers between devices, per_device(): lax.all_to_all(mixed_local, 'wide', split_axis=0, concat_axis=1, tiled=True)  5.72 us
  transfers between devices with their start and end apart: 2, of which 1 were waited for; matrix products, arithmetic and copies ran while one was open for 40% of the time, Pallas kernels for 0%

commit v1 on v0

--- a/solution.py
+++ b/solution.py
@@ -1,12 +1,457 @@
+import functools
+
 import jax
 import jax.numpy as jnp
 from jax import lax
+from jax.experimental import pallas as pl
+from jax.experimental.pallas import tpu as pltpu
 from jax.sharding import PartitionSpec as P
 
 HIGH = lax.Precision.HIGHEST
-
-
-def per_device(
+LANES = 128
+MESH = pl.DeviceIdType.MESH
+F32 = jnp.float32
+BF16 = jnp.bfloat16
+
+
+def split_two(x):
+    high = x.astype(BF16).astype(F32)
+    return high, x - high
+
+
+def kernel(
+    n_grp,
+    n_wide,
+    n_orb,
+    coeff,
+    beta,
+    blocks,
+    alpha,
+    mask,
+    source,
+    pair,
+    parity,
+    occupation,
+    coulomb,
+    out,
+    strings,
+    strings_high,
+    strings_low,
+    partner,
+    staged,
+    arrived,
+    dense,
+    picked_high,
+    picked_low,
+    applied,
+    placed,
+    padded,
+    source_t,
+    pair_t,
+    sign_t,
+    wide_c,
+    table,
+    occ,
+    left,
+    onehot,
+    m_high,
+    m_low,
+    beta_sem,
+    go_send,
+    go_recv,
+    relay_send,
+    relay_recv,
+    back_send,
+    back_recv,
+    partner_send,
+    partner_recv,
+):
+    g = lax.axis_index("grp")
+    w = lax.axis_index("wide")
+    rows, width = coeff.shape
+    cut = width // n_wide
+    exc = source.shape[0]
+    n_pair = coulomb.shape[0]
+    chunks = table.shape[1] // LANES
+    n_strings = n_grp * n_wide * rows
+    k_size = rows * LANES
+    p_size = blocks.shape[1]
+    size = beta.shape[1]
+    n_blocks = width // size
+
+    barrier = pltpu.get_barrier_semaphore()
+
+    def greet(d, _):
+        pl.semaphore_signal(
+            barrier, inc=1, device_id=(g, lax.rem(w + d, n_wide)), device_id_type=MESH
+        )
+        return 0
+
+    lax.fori_loop(1, n_wide, greet, 0)
+    for h in range(1, n_grp):
+        pl.semaphore_signal(
+            barrier, inc=1, device_id=(lax.rem(g + h, n_grp), w), device_id_type=MESH
+        )
+    fetch = pltpu.make_async_copy(beta, dense, beta_sem)
+    fetch.start()
+    pl.semaphore_wait(barrier, n_wide - 1 + n_grp - 1)
+
+    def columns(j):
+        return pl.ds(pl.multiple_of(j * cut, LANES), cut)
+
+    def go(d):
+        to = lax.rem(w + d, n_wide)
+        return pltpu.make_async_remote_copy(
+            src_ref=coeff.at[:, columns(to)],
+            dst_ref=strings.at[g * n_wide + w],
+            send_sem=go_send.at[d],
+            recv_sem=go_recv.at[d],
+            device_id=(g, to),
+            device_id_type=MESH,
+        )
+
+    def relay(d, h):
+        slot = g * n_wide + lax.rem(w - d + n_wide, n_wide)
+        return pltpu.make_async_remote_copy(
+            src_ref=strings.at[slot],
+            dst_ref=strings.at[slot],
+            send_sem=relay_send.at[h, d],
+            recv_sem=relay_recv.at[h, d],
+            device_id=(lax.rem(g + h, n_grp), w),
+            device_id_type=MESH,
+        )
+
+    def back(d):
+        to = lax.rem(w + d, n_wide)
+        return pltpu.make_async_remote_copy(
+            src_ref=staged.at[to],
+            dst_ref=arrived.at[w],
+            send_sem=back_send.at[d],
+            recv_sem=back_recv.at[d],
+            device_id=(g, to),
+            device_id_type=MESH,
+        )
+
+    def across(h):
+        return pltpu.make_async_remote_copy(
+            src_ref=coeff,
+            dst_ref=partner.at[g],
+            send_sem=partner_send.at[h],
+            recv_sem=partner_recv.at[h],
+            device_id=(lax.rem(g + h, n_grp), w),
+            device_id_type=MESH,
+        )
+
+    def start_go(d, _):
+        go(d).start()
+        return 0
+
+    lax.fori_loop(1, n_wide, start_go, 0)
+    strings[g * n_wide + w] = coeff[:, columns(w)]
+    for h in range(1, n_grp):
+        relay(0, h).start()
+
+    padded[...] = jnp.zeros_like(padded)
+    padded[0:exc, :] = source[...]
+    source_t[...] = padded[...].T
+    padded[0:exc, :] = pair[...]
+    pair_t[...] = padded[...].T
+    padded[0:exc, :] = 1 - 2 * parity[...]
+    sign_t[...] = padded[...].T.astype(F32)
+    wide_c[...] = jnp.zeros_like(wide_c)
+    wide_c[0:n_pair, 0:n_orb] = coulomb[...]
+    for c in range(chunks):
+        table[:, c * LANES : (c + 1) * LANES] = wide_c[c * LANES : (c + 1) * LANES, :].T
+    for r in range(n_orb):
+        occ[r] = jnp.broadcast_to(occupation[r : r + 1, :].astype(F32), (rows, cut))
+
+    def build(block):
+        at = pl.ds(pl.multiple_of(block * rows, rows), rows)
+        pairs = pair_t[at, :]
+        signs = sign_t[at, :]
+        which = pairs // LANES
+        lane = pairs - which * LANES
+        sublane = lax.broadcasted_iota(jnp.int32, (rows, LANES), 0)
+        for r in range(0, n_orb, 2):
+            halves = []
+            for q in (r, r + 1):
+                value = jnp.zeros((rows, LANES), F32)
+                for c in range(chunks):
+                    line = jnp.broadcast_to(
+                        table[q : q + 1, c * LANES : (c + 1) * LANES], (rows, LANES)
+                    )
+                    got = jnp.take_along_axis(line, lane, axis=1, mode="promise_in_bounds")
+                    value = jnp.where(which == c, got, value)
+                halves.append(split_two(value * signs))
+            for part in range(2):
+                base = part * n_orb * rows + r * rows
+                for a in range(rows):
+                    both = jnp.concatenate(
+                        [jnp.where(sublane == a, half[part], 0.0) for half in halves], axis=0
+                    )
+                    left[base : base + 2 * rows, a * LANES : (a + 1) * LANES] = both.astype(BF16)
+        string = lax.broadcasted_iota(jnp.int32, (n_strings, LANES), 0)
+        sources = source_t[at, :]
+        for a in range(rows):
+            hit = string == jnp.broadcast_to(sources[a : a + 1, :], (n_strings, LANES))
+            onehot[:, a * LANES : (a + 1) * LANES] = jnp.where(hit, 1.0, 0.0).astype(BF16)
+        m = lax.dot_general(
+            left[...], onehot[...], (((1,), (1,)), ((), ())), preferred_element_type=F32
+        )
+        m = m[: n_orb * rows] + m[n_orb * rows :]
+        high, low = split_two(m)
+        m_high[block] = high.astype(BF16)
+        m_low[block] = low.astype(BF16)
+
+    build(0)
+
+    def build_and_relay(d, _):
+        build(d)
+        go(d).wait_recv()
+        for h in range(1, n_grp):
+            relay(d, h).start()
+        return 0
+
+    lax.fori_loop(1, n_wide, build_and_relay, 0)
+    for h in range(1, n_grp):
+        across(h).start()
+
+    def wait_relay(d, _):
+        for h in range(1, n_grp):
+            relay(d, h).wait_recv()
+        return 0
+
+    lax.fori_loop(0, n_wide, wait_relay, 0)
+    high, low = split_two(strings[...].reshape(n_strings, cut))
+    strings_high[...] = high.astype(BF16)
+    strings_low[...] = low.astype(BF16)
+
+    def mix(to):
+        y = jnp.dot(m_high[to], strings_high[...], preferred_element_type=F32)
+        y += jnp.dot(m_low[to], strings_high[...], preferred_element_type=F32)
+        y += jnp.dot(m_high[to], strings_low[...], preferred_element_type=F32)
+        total = y[0:rows] * occ[0]
+        for r in range(1, n_orb):
+            total += y[r * rows : (r + 1) * rows] * occ[r]
+        return total
+
+    def mix_and_send(d, _):
+        to = lax.rem(w + d, n_wide)
+        staged[to] = mix(to)
+        back(d).start()
+        return 0
+
+    lax.fori_loop(1, n_wide, mix_and_send, 0)
+    arrived[w] = mix(w)
+
+    fetch.wait()
+
+    for t in range(n_blocks):
+        placed[t * rows : (t + 1) * rows, :] = coeff[:, t * size : (t + 1) * size]
+    source_hit = lax.broadcasted_iota(jnp.int32, (p_size, n_blocks), 1) == jnp.broadcast_to(
+        blocks_column(blocks, p_size), (p_size, n_blocks)
+    )
+    choose = jnp.where(source_hit, 1.0, 0.0).astype(BF16)
+    for r in range(rows):
+        high, low = split_two(placed[pl.ds(r, n_blocks, stride=rows), :])
+        picked_high[pl.ds(r, p_size, stride=rows), :] = jnp.dot(
+            choose, high.astype(BF16), preferred_element_type=F32
+        )
+        picked_low[pl.ds(r, p_size, stride=rows), :] = jnp.dot(
+            choose, low.astype(BF16), preferred_element_type=F32
+        )
+
+    def pick(k):
+        at = pl.ds(pl.multiple_of(k * rows, rows), rows)
+        high, low = picked_high[at, :], picked_low[at, :]
+        return jnp.concatenate(
+            [
+                jnp.concatenate([high, high], axis=1),
+                jnp.concatenate([low, jnp.zeros_like(low)], axis=1),
+            ],
+            axis=0,
+        )
+
+    def apply_two(i, _):
+        k = 2 * i
+        lhs = jnp.concatenate([pick(k), pick(k + 1)], axis=0).astype(BF16)
+        h0, l0 = split_two(dense[k])
+        h1, l1 = split_two(dense[k + 1])
+        rhs = jnp.concatenate(
+            [jnp.concatenate([h0, h1], axis=1), jnp.concatenate([l0, l1], axis=1)], axis=0
+        ).astype(BF16)
+        y = jnp.dot(lhs, rhs, preferred_element_type=F32)
+        applied[pl.ds(k, rows, stride=p_size), :] = y[0:rows, :size] + y[rows : 2 * rows, :size]
+        applied[pl.ds(k + 1, rows, stride=p_size), :] = (
+            y[2 * rows : 3 * rows, size:] + y[3 * rows :, size:]
+        )
+        return 0
+
+    lax.fori_loop(0, p_size // 2, apply_two, 0)
+
+    target = jnp.broadcast_to(blocks_row(blocks, p_size), (n_blocks, p_size))
+    place = jnp.where(
+        lax.broadcasted_iota(jnp.int32, (n_blocks, p_size), 0) == target, 1.0, 0.0
+    ).astype(BF16)
+    for r in range(rows):
+        high, low = split_two(applied[r * p_size : (r + 1) * p_size, :])
+        y = jnp.dot(place, high.astype(BF16), preferred_element_type=F32)
+        y += jnp.dot(place, low.astype(BF16), preferred_element_type=F32)
+        placed[pl.ds(r, n_blocks, stride=rows), :] = y
+
+    for h in range(1, n_grp):
+        across(h).wait_recv()
+    factors = []
+    for h in range(n_grp):
+        who = lax.rem(g + h, n_grp)
+        block = alpha[0, who] * mask[0, who].astype(F32)
+        factors.append(
+            [jnp.broadcast_to(block[:, s : s + 1], (rows, size)) for s in range(rows)]
+        )
+
+    def couple(t, _):
+        at = pl.ds(pl.multiple_of(t * size, size), size)
+        total = placed[pl.ds(pl.multiple_of(t * rows, rows), rows), :]
+        for h in range(n_grp):
+            if h == 0:
+                c = coeff[:, at]
+            else:
+                c = partner[lax.rem(g + h, n_grp), :, at]
+            for s in range(rows):
+                total += factors[h][s] * jnp.broadcast_to(c[s : s + 1, :], (rows, size))
+        out[:, at] = total
+        return 0
+
+    lax.fori_loop(0, n_blocks, couple, 0)
+
+    def gather_up(d, _):
+        back(d).wait_recv()
+        who = lax.rem(w - d + n_wide, n_wide)
+        out[:, columns(who)] += arrived[who]
+        return 0
+
+    out[:, columns(w)] += arrived[w]
+    lax.fori_loop(1, n_wide, gather_up, 0)
+
+    def drain(d, _):
+        go(d).wait_send()
+        back(d).wait_send()
+        for h in range(1, n_grp):
+            relay(d, h).wait_send()
+        return 0
+
+    for h in range(1, n_grp):
+        relay(0, h).wait_send()
+        across(h).wait_send()
+    lax.fori_loop(1, n_wide, drain, 0)
+
+
+def blocks_column(blocks, p_size):
+    sublane = lax.broadcasted_iota(jnp.int32, (p_size, 1), 0)
+
+    def put(k, column):
+        return jnp.where(sublane == k, blocks[0, k], column)
+
+    return lax.fori_loop(0, p_size, put, jnp.zeros((p_size, 1), jnp.int32))
+
+
+def blocks_row(blocks, p_size):
+    lane = lax.broadcasted_iota(jnp.int32, (1, p_size), 1)
+
+    def put(k, row):
+        return jnp.where(lane == k, blocks[1, k], row)
+
+    return lax.fori_loop(0, p_size, put, jnp.zeros((1, p_size), jnp.int32))
+
+
+def fused(n_grp, n_wide, args):
+    coeff, beta, _, alpha, _, source, _, _, occupation, coulomb = args
+    rows, width = coeff.shape
+    cut = width // n_wide
+    n_orb = occupation.shape[0]
+    n_pair = coulomb.shape[0]
+    n_strings = n_grp * n_wide * rows
+    table_width = -(-n_pair // LANES) * LANES
+    p_size, size = beta.shape[:2]
+    vmem = pl.BlockSpec(memory_space=pltpu.VMEM)
+    smem = pl.BlockSpec(memory_space=pltpu.SMEM)
+    scratch = [
+        pltpu.VMEM((n_grp * n_wide, rows, cut), F32),
+        pltpu.VMEM((n_strings, cut), BF16),
+        pltpu.VMEM((n_strings, cut), BF16),
+        pltpu.VMEM((n_grp, rows, width), F32),
+        pltpu.VMEM((n_wide, rows, cut), F32),
+        pltpu.VMEM((n_wide, rows, cut), F32),
+        pltpu.VMEM(beta.shape, F32),
+        pltpu.VMEM((rows * p_size, size), F32),
+        pltpu.VMEM((rows * p_size, size), F32),
+        pltpu.VMEM((rows * p_size, size), F32),
+        pltpu.VMEM((width // size * rows, size), F32),
+        pltpu.VMEM((LANES, LANES), jnp.int32),
+        pltpu.VMEM((LANES, LANES), jnp.int32),
+        pltpu.VMEM((LANES, LANES), jnp.int32),
+        pltpu.VMEM((LANES, LANES), F32),
+        pltpu.VMEM((table_width, LANES), F32),
+        pltpu.VMEM((LANES, table_width), F32),
+        pltpu.VMEM((n_orb, rows, cut), F32),
+        pltpu.VMEM((2 * n_orb * rows, rows * LANES), BF16),
+        pltpu.VMEM((n_strings, rows * LANES), BF16),
+        pltpu.VMEM((n_wide, n_orb * rows, n_strings), BF16),
+        pltpu.VMEM((n_wide, n_orb * rows, n_strings), BF16),
+        pltpu.SemaphoreType.DMA,
+        pltpu.SemaphoreType.DMA((n_wide,)),
+        pltpu.SemaphoreType.DMA((n_wide,)),
+        pltpu.SemaphoreType.DMA((n_grp, n_wide)),
+        pltpu.SemaphoreType.DMA((n_grp, n_wide)),
+        pltpu.SemaphoreType.DMA((n_wide,)),
+        pltpu.SemaphoreType.DMA((n_wide,)),
+        pltpu.SemaphoreType.DMA((n_grp,)),
+        pltpu.SemaphoreType.DMA((n_grp,)),
+    ]
+    return pl.pallas_call(
+        functools.partial(kernel, n_grp, n_wide, n_orb),
+        out_shape=jax.ShapeDtypeStruct(coeff.shape, F32),
+        in_specs=[
+            vmem,
+            pl.BlockSpec(memory_space=pl.ANY),
+            smem,
+            vmem,
+            smem,
+            vmem,
+            vmem,
+            vmem,
+            vmem,
+            vmem,
+        ],
+        out_specs=vmem,
+        scratch_shapes=scratch,
+        compiler_params=pltpu.CompilerParams(
+            collective_id=0, has_side_effects=True, vmem_limit_bytes=40 * 2**20
+        ),
+    )(*args)
+
+
+def suits(n_grp, n_wide, args):
+    coeff, beta, _, _, _, source, _, _, occupation, _ = args
+    rows, width = coeff.shape
+    n_orb = occupation.shape[0]
+    return (
+        n_grp > 1
+        and n_wide > 1
+        and rows == 8
+        and width % (n_wide * LANES) == 0
+        and beta.shape[1] == LANES
+        and beta.shape[0] % 16 == 0
+        and (width // LANES) % 16 == 0
+        and n_orb % 2 == 0
+        and source.shape[0] <= LANES
+        and source.shape[1] == LANES
+        and n_wide * rows == LANES
+        and n_grp * n_wide * rows <= 512
+    )
+
+
+def general(
     coeff,
     beta_blocks,
     block_list,
@@ -68,6 +513,12 @@
     return same_beta + same_alpha + mixed
 
 
+def per_device(n_grp, n_wide, *args):
+    if suits(n_grp, n_wide, args):
+        return fused(n_grp, n_wide, args)
+    return general(*args)
+
+
 def solution(mesh):
     in_specs = (
         P(("grp", "wide"), None),
@@ -83,5 +534,8 @@
     )
     out_specs = P(("grp", "wide"), None)
     return jax.shard_map(
-        per_device, mesh=mesh, in_specs=in_specs, out_specs=out_specs, check_vma=False
-    )
+        functools.partial(per_device, mesh.shape["grp"], mesh.shape["wide"]),
+        mesh=mesh, in_specs=in_specs,
+        out_specs=out_specs,
+        check_vma=False,
+    )

time: 154 us -> 47.4 us (0.31)
  local copies, waits for them, and re-layouts: 96.1 us -> 10.5 us
  Pallas kernels: 0 us -> 36.4 us
  other arithmetic: 16.4 us -> 0 us
  blocking collectives: 15.8 us -> 0 us
  starting transfers between devices: 13.2 us -> 0 us
  matrix products: 10.6 us -> 0 us
    gather x4 -> x0, local copies, waits for them, and re-layouts: 95.1 us -> none  [the longest x2 47.6 us: one_block(): factor = jnp.take(weights_local, pairs, axis=0)]
    pallas_call x0 -> x1, Pallas kernels: none -> 36.4 us  [fused(): pl.pallas_call(functools.partial(kernel, n_grp, n_wide, n_orb), out_shape...]
    all_gather x2 -> x0, blocking collectives: 15.8 us -> none  [the longest x1 7.91 us: per_device(): every_string = lax.all_gather(beta_major, 'grp', axis=0, tiled=True)]
    all_to_all x2 -> x0, starting transfers between devices: 13.2 us -> none  [the longest x1 7.49 us: per_device(): lax.all_to_all(coeff, 'wide', split_axis=1, concat_axis=0, tiled=True)]
    reduce_sum x1 -> x0, other arithmetic: 13.1 us -> none  [one_block(): return jnp.sum(signs[:, :, None] * factor * fetched, axis=1)]
    dot_general x5 -> x0, matrix products: 10.6 us -> none  [the longest x1 7.45 us: per_device(): applied = jnp.einsum('rpk,pkl->rpl', picked, beta_blocks, precision=HIGH)]
    unnamed x14 -> x20, local copies, waits for them, and re-layouts: 0.03 us -> 10.5 us
    and x2 -> x0, other arithmetic: 1.63 us -> none  [the longest x1 0.82 us: one_block(): factor = jnp.take(weights_local, pairs, axis=0)]
  transfers between devices with their start and end apart: 2 -> 0, of which waited for: 1 -> 0; matrix products, arithmetic and copies ran while one was open for 40% -> 0% of each run, Pallas kernels for 0% -> 0%
where the time goes in v1:
time: 47.4 us; the launch traced here: 46.9 us
  Pallas kernels  36.4 us (77%)
  local copies, waits for them, and re-layouts  10.5 us (22%)
    pallas_call x1, Pallas kernels, fused(): pl.pallas_call(functools.partial(kernel, n_grp, n_wide, n_orb), out_shape...  36.4 us
    unnamed x20, local copies, waits for them, and re-layouts  10.5 us

profile of v1, /device:TPU:0, one launch (start us, length us, event | category | flops | bytes accessed | tf_op | source)
XLA Modules:
  0.0 46.9 jit_solution(7517732861602609928)
XLA Ops:
  0.0 0.9 %copy.11.coulomb = f32[324,18]{1,0:T(8,128)S(1)} copy(f32[324,18]{0,1:T(8,128)} %param.19) | data formatting | bytes 46656 | tf_op args[9]
  0.9 0.0 copy-start
  0.9 2.8 %copy-done = f32[96,128,128]{2,1,0:T(8,128)S(1)} copy-done((f32[96,128,128]{2,1,0:T(8,128)S(1)}, f32[96,128,128]{2,1,0:T(8,128)}, u32[]{:S(2)}) %copy-start) | copy-done | bytes 6291480
  3.7 0.0 copy-start.1
  3.7 0.9 %copy-done.1 = f32[8,6144]{1,0:T(8,128)S(1)} copy-done((f32[8,6144]{1,0:T(8,128)S(1)}, f32[8,6144]{1,0:T(8,128)}, u32[]{:S(2)}) %copy-start.1) | copy-done | bytes 196632
  4.6 0.0 copy-start.2
  4.6 0.8 %copy-done.2 = s32[90,128]{1,0:T(8,128)S(1)} copy-done((s32[90,128]{1,0:T(8,128)S(1)}, s32[90,128]{1,0:T(8,128)}, u32[]{:S(2)}) %copy-start.2) | copy-done | bytes 46104
  5.4 0.0 copy-start.3
  5.4 0.8 %copy-done.3 = s32[90,128]{1,0:T(8,128)S(1)} copy-done((s32[90,128]{1,0:T(8,128)S(1)}, s32[90,128]{1,0:T(8,128)}, u32[]{:S(2)}) %copy-start.3) | copy-done | bytes 46104
  6.2 0.0 copy-start.4
  6.2 0.8 %copy-done.4 = s32[90,128]{1,0:T(8,128)S(1)} copy-done((s32[90,128]{1,0:T(8,128)S(1)}, s32[90,128]{1,0:T(8,128)}, u32[]{:S(2)}) %copy-start.4) | copy-done | bytes 46104
  7.0 0.0 copy-start.5
  7.0 0.8 %copy-done.5 = s32[18,384]{1,0:T(8,128)S(1)} copy-done((s32[18,384]{1,0:T(8,128)S(1)}, s32[18,384]{1,0:T(8,128)}, u32[]{:S(2)}) %copy-start.5) | copy-done | bytes 27672
  7.8 0.0 copy-start.6
  7.8 0.7 %copy-done.6 = f32[1,2,8,8]{3,2,1,0:T(8,128)S(1)} copy-done((f32[1,2,8,8]{3,2,1,0:T(8,128)S(1)}, f32[1,2,8,8]{3,2,1,0:T(8,128)}, u32[]{:S(2)}) %copy-start.6) | copy-done | bytes 536
  8.5 0.0 copy-start.7
  8.5 0.7 %copy-done.7 = s32[2,96]{1,0:T(2,128)S(1)} copy-done((s32[2,96]{1,0:T(2,128)S(1)}, s32[2,96]{1,0:T(2,128)}, u32[]{:S(2)}) %copy-start.7) | copy-done | bytes 792
  9.1 0.0 copy-start.8
  9.1 0.7 %copy-done.8 = s32[1,2]{1,0:T(1,128)S(1)} copy-done((s32[1,2]{1,0:T(1,128)S(1)}, s32[1,2]{1,0:T(1,128)}, u32[]{:S(2)}) %copy-start.8) | copy-done | bytes 32
  9.8 36.4 %shard_map.100 = f32[8,6144]{1,0:T(8,128)S(1)} custom-call(f32[8,6144]{1,0:T(8,128)S(1)} %copy-done.1, f32[96,128,128]{2,1,0:T(8,128)S(1)} %copy-done, s32[2,96]{1,0:T(2,128)S(1)} %copy-done.7, f32[1,2,8,8]{3,2,1,0:T(8,128)S(1)} %copy-done.6, s32[1,2]{1,0:T(1,128)S(1)} %copy-done.8, s32[90,128]{1,0:T(8,128)S(1)} %copy-done.2, s32[90,128]{1,0:T(8,128)S(1)} %copy-done.3, ...), custom_call_target="tpu_custom_call" | custom-call | tf_op jit(solution)/shard_map/pallas_call | solution.py:411
  46.2 0.7 %copy.13 = f32[8,6144]{1,0:T(8,128)} copy(f32[8,6144]{1,0:T(8,128)S(1)} %shard_map.100) | data formatting | bytes 393216
Async XLA Ops:
  0.9 2.8 %copy-start = (f32[96,128,128]{2,1,0:T(8,128)S(1)}, f32[96,128,128]{2,1,0:T(8,128)}, u32[]{:S(2)}) copy-start(f32[96,128,128]{2,1,0:T(8,128)} %beta.1) | copy-start | bytes 18874372
  3.7 0.9 %copy-start.1 = (f32[8,6144]{1,0:T(8,128)S(1)}, f32[8,6144]{1,0:T(8,128)}, u32[]{:S(2)}) copy-start(f32[8,6144]{1,0:T(8,128)} %coeff.1) | copy-start | bytes 589828
  4.6 0.8 %copy-start.2 = (s32[90,128]{1,0:T(8,128)S(1)}, s32[90,128]{1,0:T(8,128)}, u32[]{:S(2)}) copy-start(s32[90,128]{1,0:T(8,128)} %source.1) | copy-start | bytes 138244
  5.4 0.8 %copy-start.3 = (s32[90,128]{1,0:T(8,128)S(1)}, s32[90,128]{1,0:T(8,128)}, u32[]{:S(2)}) copy-start(s32[90,128]{1,0:T(8,128)} %pair.1) | copy-start | bytes 138244
  6.2 0.8 %copy-start.4 = (s32[90,128]{1,0:T(8,128)S(1)}, s32[90,128]{1,0:T(8,128)}, u32[]{:S(2)}) copy-start(s32[90,128]{1,0:T(8,128)} %parity.1) | copy-start | bytes 138244
  7.0 0.8 %copy-start.5 = (s32[18,384]{1,0:T(8,128)S(1)}, s32[18,384]{1,0:T(8,128)}, u32[]{:S(2)}) copy-start(s32[18,384]{1,0:T(8,128)} %occupation.1) | copy-start | bytes 82948
  7.8 0.7 %copy-start.6 = (f32[1,2,8,8]{3,2,1,0:T(8,128)S(1)}, f32[1,2,8,8]{3,2,1,0:T(8,128)}, u32[]{:S(2)}) copy-start(f32[1,2,8,8]{3,2,1,0:T(8,128)} %alpha.1) | copy-start | bytes 1540
  8.5 0.7 %copy-start.7 = (s32[2,96]{1,0:T(2,128)S(1)}, s32[2,96]{1,0:T(2,128)}, u32[]{:S(2)}) copy-start(s32[2,96]{1,0:T(2,128)} %blocks.1) | copy-start | bytes 2308
  9.1 0.7 %copy-start.8 = (s32[1,2]{1,0:T(1,128)S(1)}, s32[1,2]{1,0:T(1,128)}, u32[]{:S(2)}) copy-start(s32[1,2]{1,0:T(1,128)} %mask.1) | copy-start | bytes 28

commit v2 on v0

--- a/solution.py
+++ b/solution.py
@@ -1,12 +1,547 @@
+import functools
+
 import jax
 import jax.numpy as jnp
 from jax import lax
+from jax.experimental import pallas as pl
+from jax.experimental.pallas import tpu as pltpu
 from jax.sharding import PartitionSpec as P
 
 HIGH = lax.Precision.HIGHEST
-
-
-def per_device(
+LANES = 128
+MESH = pl.DeviceIdType.MESH
+F32 = jnp.float32
+BF16 = jnp.bfloat16
+
+
+def split_two(x):
+    high = x.astype(BF16).astype(F32)
+    return high, x - high
+
+
+def split_narrow(x):
+    high = x.astype(BF16)
+    return high, (x - high.astype(F32)).astype(BF16)
+
+
+def kernel(
+    n_grp,
+    n_wide,
+    coeff_hbm,
+    beta_hbm,
+    blocks_hbm,
+    alpha_hbm,
+    mask_hbm,
+    source_hbm,
+    pair_hbm,
+    parity_hbm,
+    occupation_hbm,
+    coulomb_hbm,
+    out,
+    coeff,
+    dense,
+    blocks,
+    alpha,
+    mask,
+    source,
+    pair,
+    parity,
+    occupation,
+    coulomb,
+    strings,
+    strings_three,
+    partner,
+    staged,
+    arrived,
+    picked_high,
+    picked_low,
+    applied,
+    placed,
+    padded,
+    source_pad,
+    pair_t,
+    sign_t,
+    table,
+    occ,
+    left,
+    onehot,
+    m_three,
+    in_sem,
+    go_send,
+    go_recv,
+    relay_send,
+    relay_recv,
+    mate_send,
+    mate_recv,
+    occ_send,
+    occ_recv,
+    back_send,
+    back_recv,
+    partner_send,
+    partner_recv,
+):
+    g = lax.axis_index("grp")
+    w = lax.axis_index("wide")
+    chip = w // 2
+    core = lax.rem(w, 2)
+    n_chip = n_wide // 2
+    mate = (g, 2 * chip + 1 - core)
+    rows, width = coeff.shape
+    cut = width // n_chip
+    exc = source.shape[0]
+    n_orb, n_pair = coulomb.shape
+    chunks = table.shape[1] // LANES
+    n_strings = n_grp * n_wide * rows
+    n_m = n_orb * rows
+    p_size, size = dense.shape[:2]
+    n_blocks = width // size
+
+    barrier = pltpu.get_barrier_semaphore()
+
+    def greet(d, _):
+        to = 2 * lax.rem(chip + d, n_chip) + core
+        pl.semaphore_signal(barrier, inc=1, device_id=(g, to), device_id_type=MESH)
+        return 0
+
+    lax.fori_loop(1, n_chip, greet, 0)
+    for h in range(1, n_grp):
+        pl.semaphore_signal(
+            barrier, inc=1, device_id=(lax.rem(g + h, n_grp), w), device_id_type=MESH
+        )
+    pl.semaphore_signal(barrier, inc=1, device_id=mate, device_id_type=MESH)
+
+    fetches = [
+        pltpu.make_async_copy(a, b, in_sem.at[i])
+        for i, (a, b) in enumerate(
+            (
+                (pair_hbm, pair),
+                (parity_hbm, parity),
+                (source_hbm, source),
+                (coulomb_hbm, coulomb),
+                (occupation_hbm, occupation.at[core]),
+                (coeff_hbm, coeff),
+                (blocks_hbm, blocks),
+                (alpha_hbm, alpha),
+                (mask_hbm, mask),
+                (beta_hbm, dense),
+            )
+        )
+    ]
+    for fetch in fetches:
+        fetch.start()
+    pl.semaphore_wait(barrier, n_chip - 1 + n_grp)
+
+    def columns(j):
+        return pl.ds(pl.multiple_of(j * cut, LANES), cut)
+
+    def slot(d, h):
+        group = lax.rem(g - h + n_grp, n_grp)
+        return group * n_wide + 2 * lax.rem(chip - d + n_chip, n_chip) + core
+
+    def go(d):
+        to = lax.rem(chip + d, n_chip)
+        return pltpu.make_async_remote_copy(
+            src_ref=coeff_hbm.at[:, columns(to)],
+            dst_ref=strings.at[g * n_wide + w],
+            send_sem=go_send.at[d],
+            recv_sem=go_recv.at[d],
+            device_id=(g, 2 * to + core),
+            device_id_type=MESH,
+        )
+
+    def relay(d, h):
+        return pltpu.make_async_remote_copy(
+            src_ref=strings.at[slot(d, 0)],
+            dst_ref=strings.at[slot(d, 0)],
+            send_sem=relay_send.at[h, d],
+            recv_sem=relay_recv.at[h, d],
+            device_id=(lax.rem(g + h, n_grp), w),
+            device_id_type=MESH,
+        )
+
+    def to_mate(d, h):
+        return pltpu.make_async_remote_copy(
+            src_ref=strings.at[slot(d, h)],
+            dst_ref=strings.at[slot(d, h)],
+            send_sem=mate_send.at[h, d],
+            recv_sem=mate_recv.at[h, d],
+            device_id=mate,
+            device_id_type=MESH,
+        )
+
+    occ_copy = pltpu.make_async_remote_copy(
+        src_ref=occupation_hbm,
+        dst_ref=occupation.at[core],
+        send_sem=occ_send,
+        recv_sem=occ_recv,
+        device_id=mate,
+        device_id_type=MESH,
+    )
+
+    def back(d):
+        to = lax.rem(chip + d, n_chip)
+        return pltpu.make_async_remote_copy(
+            src_ref=staged.at[to],
+            dst_ref=arrived.at[chip],
+            send_sem=back_send.at[d],
+            recv_sem=back_recv.at[d],
+            device_id=(g, 2 * to + core),
+            device_id_type=MESH,
+        )
+
+    def across(h):
+        return pltpu.make_async_remote_copy(
+            src_ref=coeff_hbm,
+            dst_ref=partner.at[g],
+            send_sem=partner_send.at[h],
+            recv_sem=partner_recv.at[h],
+            device_id=(lax.rem(g + h, n_grp), w),
+            device_id_type=MESH,
+        )
+
+    def start_go(d, _):
+        go(d).start()
+        return 0
+
+    lax.fori_loop(1, n_chip, start_go, 0)
+    occ_copy.start()
+
+    padded[...] = jnp.zeros_like(padded)
+    onehot[...] = jnp.zeros_like(onehot)
+    table[...] = jnp.zeros_like(table)
+    fetches[0].wait()
+    padded[0:exc, :] = pair[...]
+    pair_t[...] = padded[...].T
+    fetches[1].wait()
+    padded[0:exc, :] = 1 - 2 * parity[...]
+    sign_t[...] = padded[...].T.astype(F32)
+    source_pad[...] = jnp.zeros_like(source_pad)
+    fetches[2].wait()
+    source_pad[0:exc, :] = source[...]
+    fetches[3].wait()
+    table[0:n_orb, 0:n_pair] = coulomb[...]
+    fetches[5].wait()
+    strings[g * n_wide + w] = coeff[:, columns(chip)]
+    partner[g] = coeff[...]
+    for h in range(1, n_grp):
+        relay(0, h).start()
+    to_mate(0, 0).start()
+
+    def build(to):
+        block = 2 * to + core
+        at = pl.ds(pl.multiple_of(block * rows, rows), rows)
+        pairs = pair_t[at, :]
+        signs = sign_t[at, :]
+        which = pairs // LANES
+        lane = pairs - which * LANES
+        sublane = lax.broadcasted_iota(jnp.int32, (rows, LANES), 0)
+        string = lax.broadcasted_iota(jnp.int32, (16, n_strings), 1)
+        for a in range(rows):
+            column = jnp.full((rows, LANES), block * rows + a, jnp.int32)
+            for e in range(0, exc, 16):
+                pieces = [
+                    jnp.take_along_axis(
+                        source_pad[e + f : e + f + rows, :],
+                        column,
+                        axis=1,
+                        mode="promise_in_bounds",
+                    )
+                    for f in (0, 8)
+                ]
+                both = jnp.concatenate(pieces, axis=0)
+                full = jnp.concatenate([both] * (n_strings // LANES), axis=1)
+                onehot[a * LANES + e : a * LANES + e + 16, :] = jnp.where(
+                    full == string, 1.0, 0.0
+                ).astype(BF16)
+        for r in range(0, n_orb, 2):
+            halves = []
+            for q in (r, r + 1):
+                value = None
+                for c in range(chunks):
+                    line = jnp.broadcast_to(
+                        table[q : q + 1, c * LANES : (c + 1) * LANES], (rows, LANES)
+                    )
+                    got = jnp.take_along_axis(line, lane, axis=1, mode="promise_in_bounds")
+                    value = got if value is None else jnp.where(which == c, got, value)
+                halves.append(split_two(value * signs))
+            for part in range(2):
+                base = part * n_m + r * rows
+                for a in range(rows):
+                    both = jnp.concatenate(
+                        [jnp.where(sublane == a, half[part], 0.0) for half in halves], axis=0
+                    )
+                    left[base : base + 2 * rows, a * LANES : (a + 1) * LANES] = both.astype(BF16)
+        m = jnp.dot(left[...], onehot[...], preferred_element_type=F32)
+        high, low = split_narrow(m[:n_m] + m[n_m:])
+        m_three[to, :, 0:n_strings] = high
+        m_three[to, :, n_strings : 2 * n_strings] = low
+        m_three[to, :, 2 * n_strings :] = high
+
+    build(0)
+
+    def build_and_pass(d, _):
+        build(d)
+        go(d).wait_recv()
+        for h in range(1, n_grp):
+            relay(d, h).start()
+        to_mate(d, 0).start()
+        return 0
+
+    lax.fori_loop(1, n_chip, build_and_pass, 0)
+    for h in range(1, n_grp):
+        across(h).start()
+
+    fetches[6].wait()
+    padded[0:2, 0:p_size] = blocks[...]
+    blocks_t = padded[...].T
+    for t in range(n_blocks):
+        placed[t * rows : (t + 1) * rows, :] = coeff[:, t * size : (t + 1) * size]
+    choose = jnp.where(
+        lax.broadcasted_iota(jnp.int32, (p_size, n_blocks), 1)
+        == jnp.broadcast_to(blocks_t[0:p_size, 0:1], (p_size, n_blocks)),
+        1.0,
+        0.0,
+    ).astype(BF16)
+    for r in range(rows):
+        high, low = split_narrow(placed[pl.ds(r, n_blocks, stride=rows), :])
+        both = jnp.dot(
+            choose, jnp.concatenate([high, low], axis=1), preferred_element_type=F32
+        )
+        picked_high[pl.ds(r, p_size, stride=rows), :] = both[:, :size]
+        picked_low[pl.ds(r, p_size, stride=rows), :] = both[:, size:]
+    fetches[9].wait()
+
+    def pick(k):
+        at = pl.ds(pl.multiple_of(k * rows, rows), rows)
+        high, low = picked_high[at, :], picked_low[at, :]
+        return [
+            jnp.concatenate([high, high], axis=1),
+            jnp.concatenate([low, jnp.zeros_like(low)], axis=1),
+        ]
+
+    share = p_size // n_chip
+
+    def dense_and_pass(d, _):
+        results = []
+        for i in range(0, share, 2):
+            k = d * share + i
+            lhs = jnp.concatenate(pick(k) + pick(k + 1), axis=0).astype(BF16)
+            h0, l0 = split_narrow(dense[k])
+            h1, l1 = split_narrow(dense[k + 1])
+            rhs = jnp.concatenate(
+                [jnp.concatenate([h0, h1], axis=1), jnp.concatenate([l0, l1], axis=1)], axis=0
+            )
+            y = jnp.dot(lhs, rhs, preferred_element_type=F32)
+            results.append(y[0:rows, :size] + y[rows : 2 * rows, :size])
+            results.append(y[2 * rows : 3 * rows, size:] + y[3 * rows :, size:])
+        for i, result in enumerate(results):
+            applied[pl.ds(d * share + i, rows, stride=p_size), :] = result
+        for h in range(1, n_grp):
+            relay(d, h).wait_recv()
+            to_mate(d, h).start()
+        return 0
+
+    lax.fori_loop(0, n_chip, dense_and_pass, 0)
+
+    fetches[4].wait()
+    occ_copy.wait_recv()
+    half = occupation.shape[2]
+    for r in range(n_orb):
+        for q in range(2):
+            occ[r, :, q * half : (q + 1) * half] = jnp.broadcast_to(
+                occupation[q, r : r + 1, :].astype(F32), (rows, half)
+            )
+
+    def wait_mate(d, _):
+        for h in range(n_grp):
+            to_mate(d, h).wait_recv()
+        return 0
+
+    lax.fori_loop(0, n_chip, wait_mate, 0)
+    high, low = split_narrow(strings[...].reshape(n_strings, cut))
+    strings_three[0:n_strings, :] = high
+    strings_three[n_strings : 2 * n_strings, :] = high
+    strings_three[2 * n_strings :, :] = low
+
+    def mix_two(i, _):
+        d = 2 * i + 1
+        tos = [lax.rem(chip + d, n_chip), lax.rem(chip + d + 1, n_chip)]
+        y = jnp.dot(
+            jnp.concatenate([m_three[to] for to in tos], axis=0),
+            strings_three[...],
+            preferred_element_type=F32,
+        )
+        for q in range(2):
+            total = y[q * n_m : q * n_m + rows] * occ[0]
+            for r in range(1, n_orb):
+                total += y[q * n_m + r * rows : q * n_m + (r + 1) * rows] * occ[r]
+            staged[tos[q]] = total
+        back(d).start()
+
+        @pl.when(d + 1 < n_chip)
+        def _():
+            back(d + 1).start()
+
+        return 0
+
+    lax.fori_loop(0, n_chip // 2, mix_two, 0)
+
+    place = jnp.where(
+        lax.broadcasted_iota(jnp.int32, (n_blocks, p_size), 0)
+        == jnp.broadcast_to(blocks[1:2, :], (n_blocks, p_size)),
+        1.0,
+        0.0,
+    ).astype(BF16)
+    place = jnp.concatenate([place, place], axis=1)
+    for r in range(0, rows, 2):
+        parts = [split_narrow(applied[q * p_size : (q + 1) * p_size, :]) for q in (r, r + 1)]
+        both = jnp.concatenate(
+            [jnp.concatenate([part[i] for part in parts], axis=1) for i in range(2)], axis=0
+        )
+        y = jnp.dot(place, both, preferred_element_type=F32)
+        placed[pl.ds(r, n_blocks, stride=rows), :] = y[:, :size]
+        placed[pl.ds(r + 1, n_blocks, stride=rows), :] = y[:, size:]
+
+    fetches[7].wait()
+    fetches[8].wait()
+    factors = []
+    for h in range(n_grp):
+        block = alpha[0, h] * mask[0:1, h : h + 1].astype(F32)
+        factors.append(
+            [jnp.broadcast_to(block[:, s : s + 1], (rows, size)) for s in range(rows)]
+        )
+    for h in range(1, n_grp):
+        across(h).wait_recv()
+
+    def couple(i, _):
+        for j in range(4):
+            t = 4 * i + j
+            at = pl.ds(pl.multiple_of(t * size, size), size)
+            total = placed[pl.ds(pl.multiple_of(t * rows, rows), rows), :]
+            for h in range(n_grp):
+                c = partner[h, :, at]
+                for s in range(rows):
+                    total += factors[h][s] * jnp.broadcast_to(c[s : s + 1, :], (rows, size))
+            out[:, at] = total
+        return 0
+
+    lax.fori_loop(0, n_blocks // 4, couple, 0)
+
+    out[:, columns(chip)] += staged[chip]
+
+    def gather_up(d, _):
+        back(d).wait_recv()
+        who = lax.rem(chip - d + n_chip, n_chip)
+        out[:, columns(who)] += arrived[who]
+        return 0
+
+    lax.fori_loop(1, n_chip, gather_up, 0)
+
+    def drain(d, _):
+        go(d).wait_send()
+        back(d).wait_send()
+        return 0
+
+    lax.fori_loop(1, n_chip, drain, 0)
+
+    def drain_passed(d, _):
+        to_mate(d, 0).wait_send()
+        for h in range(1, n_grp):
+            relay(d, h).wait_send()
+            to_mate(d, h).wait_send()
+        return 0
+
+    lax.fori_loop(0, n_chip, drain_passed, 0)
+    occ_copy.wait_send()
+    for h in range(1, n_grp):
+        across(h).wait_send()
+
+
+def fused(n_grp, n_wide, args):
+    coeff, beta, blocks, alpha, mask, source, pair, parity, occupation, coulomb = args
+    coulomb = coulomb.T
+    rows, width = coeff.shape
+    n_chip = n_wide // 2
+    cut = width // n_chip
+    n_orb, n_pair = coulomb.shape
+    n_m = n_orb * rows
+    n_strings = n_grp * n_wide * rows
+    table_width = -(-n_pair // LANES) * LANES
+    p_size, size = beta.shape[:2]
+    operands = (coeff, beta, blocks, alpha, mask, source, pair, parity, occupation, coulomb)
+    landing = [pltpu.VMEM(x.shape, x.dtype) for x in operands]
+    landing[8] = pltpu.VMEM((2,) + occupation.shape, occupation.dtype)
+    dma = pltpu.SemaphoreType.DMA
+    scratch = landing + [
+        pltpu.VMEM((n_grp * n_wide, rows, cut), F32),
+        pltpu.VMEM((3 * n_strings, cut), BF16),
+        pltpu.VMEM((n_grp, rows, width), F32),
+        pltpu.VMEM((n_chip, rows, cut), F32),
+        pltpu.VMEM((n_chip, rows, cut), F32),
+        pltpu.VMEM((rows * p_size, size), F32),
+        pltpu.VMEM((rows * p_size, size), F32),
+        pltpu.VMEM((rows * p_size, size), F32),
+        pltpu.VMEM((width // size * rows, size), F32),
+        pltpu.VMEM((LANES, LANES), jnp.int32),
+        pltpu.VMEM((LANES, LANES), jnp.int32),
+        pltpu.VMEM((LANES, LANES), jnp.int32),
+        pltpu.VMEM((LANES, LANES), F32),
+        pltpu.VMEM((-(-n_orb // 8) * 8, table_width), F32),
+        pltpu.VMEM((n_orb, rows, cut), F32),
+        pltpu.VMEM((2 * n_m, rows * LANES), BF16),
+        pltpu.VMEM((rows * LANES, n_strings), BF16),
+        pltpu.VMEM((n_chip, n_m, 3 * n_strings), BF16),
+        dma((len(operands),)),
+        dma((n_chip,)),
+        dma((n_chip,)),
+        dma((n_grp, n_chip)),
+        dma((n_grp, n_chip)),
+        dma((n_grp, n_chip)),
+        dma((n_grp, n_chip)),
+        dma,
+        dma,
+        dma((n_chip,)),
+        dma((n_chip,)),
+        dma((n_grp,)),
+        dma((n_grp,)),
+    ]
+    return pl.pallas_call(
+        functools.partial(kernel, n_grp, n_wide),
+        out_shape=jax.ShapeDtypeStruct(coeff.shape, F32),
+        in_specs=[pl.BlockSpec(memory_space=pltpu.HBM)] * len(operands),
+        out_specs=pl.BlockSpec(memory_space=pltpu.VMEM),
+        scratch_shapes=scratch,
+        compiler_params=pltpu.CompilerParams(
+            collective_id=0, has_side_effects=True, vmem_limit_bytes=64 * 2**20 - 2**16
+        ),
+    )(*operands)
+
+
+def suits(n_grp, n_wide, args):
+    coeff, beta, _, _, _, source, _, _, occupation, _ = args
+    rows, width = coeff.shape
+    n_orb = occupation.shape[0]
+    n_strings = n_grp * n_wide * rows
+    return (
+        n_grp > 1
+        and n_wide > 2
+        and n_wide % 4 == 0
+        and rows == 8
+        and width % (n_wide * LANES) == 0
+        and beta.shape[1] == LANES
+        and beta.shape[0] % (2 * n_wide // 2) == 0
+        and beta.shape[0] <= LANES
+        and width // LANES % 16 == 0
+        and n_orb % 2 == 0
+        and source.shape[0] <= LANES
+        and source.shape[1] == LANES
+        and n_wide * rows == LANES
+        and n_strings % LANES == 0
+        and n_strings <= 512
+    )
+
+
+def general(
     coeff,
     beta_blocks,
     block_list,
@@ -68,6 +603,12 @@
     return same_beta + same_alpha + mixed
 
 
+def per_device(n_grp, n_wide, *args):
+    if suits(n_grp, n_wide, args):
+        return fused(n_grp, n_wide, args)
+    return general(*args)
+
+
 def solution(mesh):
     in_specs = (
         P(("grp", "wide"), None),
@@ -83,5 +624,8 @@
     )
     out_specs = P(("grp", "wide"), None)
     return jax.shard_map(
-        per_device, mesh=mesh, in_specs=in_specs, out_specs=out_specs, check_vma=False
+        functools.partial(per_device, mesh.shape["grp"], mesh.shape["wide"]),
+        mesh=mesh, in_specs=in_specs,
+        out_specs=out_specs,
+        check_vma=False,
     )

time: 154 us -> 26.8 us (0.17)
  local copies, waits for them, and re-layouts: 96.1 us -> 1.62 us
  Pallas kernels: 0 us -> 25 us
  other arithmetic: 16.4 us -> 0 us
  blocking collectives: 15.8 us -> 0 us
  starting transfers between devices: 13.2 us -> 0 us
  matrix products: 10.6 us -> 0 us
    gather x4 -> x0, local copies, waits for them, and re-layouts: 95.1 us -> none  [the longest x2 47.6 us: one_block(): factor = jnp.take(weights_local, pairs, axis=0)]
    pallas_call x0 -> x1, Pallas kernels: none -> 25 us  [fused(): pl.pallas_call(functools.partial(kernel, n_grp, n_wide), out_shape=jax.Sh...]
    all_gather x2 -> x0, blocking collectives: 15.8 us -> none  [the longest x1 7.91 us: per_device(): every_string = lax.all_gather(beta_major, 'grp', axis=0, tiled=True)]
    all_to_all x2 -> x0, starting transfers between devices: 13.2 us -> none  [the longest x1 7.49 us: per_device(): lax.all_to_all(coeff, 'wide', split_axis=1, concat_axis=0, tiled=True)]
    reduce_sum x1 -> x0, other arithmetic: 13.1 us -> none  [one_block(): return jnp.sum(signs[:, :, None] * factor * fetched, axis=1)]
    dot_general x5 -> x0, matrix products: 10.6 us -> none  [the longest x1 7.45 us: per_device(): applied = jnp.einsum('rpk,pkl->rpl', picked, beta_blocks, precision=HIGH)]
    and x2 -> x0, other arithmetic: 1.63 us -> none  [the longest x1 0.82 us: one_block(): factor = jnp.take(weights_local, pairs, axis=0)]
    select_n x2 -> x0, other arithmetic: 1.62 us -> none  [the longest x1 0.81 us: one_block(): factor = jnp.take(weights_local, pairs, axis=0)]
  transfers between devices with their start and end apart: 2 -> 0, of which waited for: 1 -> 0; matrix products, arithmetic and copies ran while one was open for 40% -> 0% of each run, Pallas kernels for 0% -> 0%
where the time goes in v2:
time: 26.8 us; the launch traced here: 26.6 us
  Pallas kernels  25 us (93%)
  local copies, waits for them, and re-layouts  1.62 us (6%)
    pallas_call x1, Pallas kernels, fused(): pl.pallas_call(functools.partial(kernel, n_grp, n_wide), out_shape=jax.Sh...  25 us
    unnamed x1, local copies, waits for them, and re-layouts  1.62 us

profile of v2, /device:TPU:0, one launch (start us, length us, event | category | flops | bytes accessed | tf_op | source)
XLA Modules:
  0.0 26.6 jit_solution(459994401142258253)
XLA Ops:
  0.0 25.0 %shard_map.100 = f32[8,6144]{1,0:T(8,128)} custom-call(f32[8,6144]{1,0:T(8,128)} %coeff_hbm.1, f32[96,128,128]{2,1,0:T(8,128)} %beta_hbm.1, s32[2,96]{1,0:T(2,128)} %blocks_hbm.1, f32[1,2,8,8]{3,2,1,0:T(8,128)} %alpha_hbm.1, s32[1,2]{1,0:T(1,128)} %mask_hbm.1, s32[90,128]{1,0:T(8,128)} %source_hbm.1, s32[90,128]{1,0:T(8,128)} %pair_hbm.1, ...), custom_call_target="tpu_custom_call" | custom-call | tf_op jit(solution)/shard_map/pallas_call | solution.py:508
  25.0 1.6 %copy.12 = f32[8,6144]{1,0:T(8,128)} copy(f32[8,6144]{1,0:T(8,128)} %shard_map.100) | data formatting | bytes 393216

commit v3 on v2

--- a/solution.py
+++ b/solution.py
@@ -37,7 +37,8 @@
     parity_hbm,
     occupation_hbm,
     coulomb_hbm,
-    out,
+    same,
+    mixed,
     coeff,
     dense,
     blocks,
@@ -52,21 +53,21 @@
     strings_three,
     partner,
     staged,
-    arrived,
-    picked_high,
-    picked_low,
+    same_vmem,
+    tiles,
+    blocks_smem,
     applied,
     placed,
     padded,
     source_pad,
     pair_t,
     sign_t,
+    coulomb_pad,
     table,
     occ,
-    left,
-    onehot,
     m_three,
     in_sem,
+    out_sem,
     go_send,
     go_recv,
     relay_send,
@@ -90,9 +91,10 @@
     cut = width // n_chip
     exc = source.shape[0]
     n_orb, n_pair = coulomb.shape
-    chunks = table.shape[1] // LANES
+    chunks = table.shape[0]
     n_strings = n_grp * n_wide * rows
-    n_m = n_orb * rows
+    n_r = -(-n_orb // 4) * 8
+    n_m = rows // 2 * n_r
     p_size, size = dense.shape[:2]
     n_blocks = width // size
 
@@ -124,6 +126,7 @@
                 (alpha_hbm, alpha),
                 (mask_hbm, mask),
                 (beta_hbm, dense),
+                (blocks_hbm, blocks_smem),
             )
         )
     ]
@@ -182,7 +185,7 @@
         to = lax.rem(chip + d, n_chip)
         return pltpu.make_async_remote_copy(
             src_ref=staged.at[to],
-            dst_ref=arrived.at[chip],
+            dst_ref=mixed.at[:, columns(chip)],
             send_sem=back_send.at[d],
             recv_sem=back_recv.at[d],
             device_id=(g, 2 * to + core),
@@ -207,7 +210,7 @@
     occ_copy.start()
 
     padded[...] = jnp.zeros_like(padded)
-    onehot[...] = jnp.zeros_like(onehot)
+    occ[...] = jnp.zeros_like(occ)
     table[...] = jnp.zeros_like(table)
     fetches[0].wait()
     padded[0:exc, :] = pair[...]
@@ -219,7 +222,12 @@
     fetches[2].wait()
     source_pad[0:exc, :] = source[...]
     fetches[3].wait()
-    table[0:n_orb, 0:n_pair] = coulomb[...]
+    coulomb_pad[...] = jnp.zeros_like(coulomb_pad)
+    coulomb_pad[:, 0:n_pair] = coulomb[...]
+    for q in range(2):
+        for c in range(chunks):
+            line = coulomb_pad[:, c * LANES : (c + 1) * LANES]
+            table[c, pl.ds(q, n_orb, stride=2), :] = line
     fetches[5].wait()
     strings[g * n_wide + w] = coeff[:, columns(chip)]
     partner[g] = coeff[...]
@@ -230,90 +238,97 @@
     def build(to):
         block = 2 * to + core
         at = pl.ds(pl.multiple_of(block * rows, rows), rows)
-        pairs = pair_t[at, :]
-        signs = sign_t[at, :]
-        which = pairs // LANES
-        lane = pairs - which * LANES
         sublane = lax.broadcasted_iota(jnp.int32, (rows, LANES), 0)
+        odd = sublane - sublane // 2 * 2 == 1
         string = lax.broadcasted_iota(jnp.int32, (16, n_strings), 1)
-        for a in range(rows):
-            column = jnp.full((rows, LANES), block * rows + a, jnp.int32)
-            for e in range(0, exc, 16):
-                pieces = [
-                    jnp.take_along_axis(
-                        source_pad[e + f : e + f + rows, :],
-                        column,
+        all_pairs = pair_t[at, :]
+        all_signs = sign_t[at, :]
+
+        def of_two(x, a):
+            return jnp.where(
+                odd,
+                jnp.broadcast_to(x[a + 1 : a + 2, :], (rows, LANES)),
+                jnp.broadcast_to(x[a : a + 1, :], (rows, LANES)),
+            )
+
+        found = []
+        for a in range(0, rows, 2):
+            hits = []
+            for b in (a, a + 1):
+                column = jnp.full((rows, LANES), block * rows + b, jnp.int32)
+                for e in range(0, LANES, 16):
+                    if e >= exc:
+                        hits.append(jnp.zeros((16, n_strings), BF16))
+                        continue
+                    pieces = [
+                        jnp.take_along_axis(
+                            source_pad[e + f : e + f + rows, :],
+                            column,
+                            axis=1,
+                            mode="promise_in_bounds",
+                        )
+                        for f in (0, 8)
+                    ]
+                    both = jnp.concatenate(pieces, axis=0)
+                    full = jnp.concatenate([both] * (n_strings // LANES), axis=1)
+                    hits.append(jnp.where(full == string, 1.0, 0.0).astype(BF16))
+            pairs = of_two(all_pairs, a)
+            signs = of_two(all_signs, a)
+            which = pairs // LANES
+            lane = pairs - which * LANES
+            parts = [[], []]
+            for r in range(0, n_r, rows):
+                value = None
+                for c in range(chunks):
+                    got = jnp.take_along_axis(
+                        table[c, r : r + rows, :],
+                        lane,
                         axis=1,
                         mode="promise_in_bounds",
                     )
-                    for f in (0, 8)
-                ]
-                both = jnp.concatenate(pieces, axis=0)
-                full = jnp.concatenate([both] * (n_strings // LANES), axis=1)
-                onehot[a * LANES + e : a * LANES + e + 16, :] = jnp.where(
-                    full == string, 1.0, 0.0
-                ).astype(BF16)
-        for r in range(0, n_orb, 2):
-            halves = []
-            for q in (r, r + 1):
-                value = None
-                for c in range(chunks):
-                    line = jnp.broadcast_to(
-                        table[q : q + 1, c * LANES : (c + 1) * LANES], (rows, LANES)
+                    value = got if value is None else jnp.where(which == c, got, value)
+                for part, half in zip(parts, split_two(value * signs)):
+                    part.append(
+                        jnp.concatenate(
+                            [jnp.where(odd, 0.0, half), jnp.where(odd, half, 0.0)], axis=1
+                        )
                     )
-                    got = jnp.take_along_axis(line, lane, axis=1, mode="promise_in_bounds")
-                    value = got if value is None else jnp.where(which == c, got, value)
-                halves.append(split_two(value * signs))
-            for part in range(2):
-                base = part * n_m + r * rows
-                for a in range(rows):
-                    both = jnp.concatenate(
-                        [jnp.where(sublane == a, half[part], 0.0) for half in halves], axis=0
-                    )
-                    left[base : base + 2 * rows, a * LANES : (a + 1) * LANES] = both.astype(BF16)
-        m = jnp.dot(left[...], onehot[...], preferred_element_type=F32)
-        high, low = split_narrow(m[:n_m] + m[n_m:])
-        m_three[to, :, 0:n_strings] = high
-        m_three[to, :, n_strings : 2 * n_strings] = low
-        m_three[to, :, 2 * n_strings :] = high
-
-    build(0)
-
-    def build_and_pass(d, _):
-        build(d)
+            left = jnp.concatenate(parts[0] + parts[1], axis=0).astype(BF16)
+            m = jnp.dot(left, jnp.concatenate(hits, axis=0), preferred_element_type=F32)
+            found.append(m[:n_r] + m[n_r:])
+        return split_narrow(jnp.concatenate(found, axis=0))
+
+    def build_and_pass(i, _):
+        d = 2 * i
+        for to, (high, low) in [(q, build(q)) for q in (d, d + 1)]:
+            m_three[to, :, 0:n_strings] = high
+            m_three[to, :, n_strings : 2 * n_strings] = low
+            m_three[to, :, 2 * n_strings :] = high
+
+        @pl.when(i > 0)
+        def _():
+            pass_on(d)
+
+        pass_on(d + 1)
+        return 0
+
+    def pass_on(d):
         go(d).wait_recv()
         for h in range(1, n_grp):
             relay(d, h).start()
         to_mate(d, 0).start()
-        return 0
-
-    lax.fori_loop(1, n_chip, build_and_pass, 0)
+
+    lax.fori_loop(0, n_chip // 2, build_and_pass, 0)
     for h in range(1, n_grp):
         across(h).start()
 
-    fetches[6].wait()
-    padded[0:2, 0:p_size] = blocks[...]
-    blocks_t = padded[...].T
+    fetches[10].wait()
     for t in range(n_blocks):
-        placed[t * rows : (t + 1) * rows, :] = coeff[:, t * size : (t + 1) * size]
-    choose = jnp.where(
-        lax.broadcasted_iota(jnp.int32, (p_size, n_blocks), 1)
-        == jnp.broadcast_to(blocks_t[0:p_size, 0:1], (p_size, n_blocks)),
-        1.0,
-        0.0,
-    ).astype(BF16)
-    for r in range(rows):
-        high, low = split_narrow(placed[pl.ds(r, n_blocks, stride=rows), :])
-        both = jnp.dot(
-            choose, jnp.concatenate([high, low], axis=1), preferred_element_type=F32
-        )
-        picked_high[pl.ds(r, p_size, stride=rows), :] = both[:, :size]
-        picked_low[pl.ds(r, p_size, stride=rows), :] = both[:, size:]
+        tiles[t] = coeff[:, t * size : (t + 1) * size]
     fetches[9].wait()
 
     def pick(k):
-        at = pl.ds(pl.multiple_of(k * rows, rows), rows)
-        high, low = picked_high[at, :], picked_low[at, :]
+        high, low = split_two(tiles[blocks_smem[0, k]])
         return [
             jnp.concatenate([high, high], axis=1),
             jnp.concatenate([low, jnp.zeros_like(low)], axis=1),
@@ -346,11 +361,12 @@
     fetches[4].wait()
     occ_copy.wait_recv()
     half = occupation.shape[2]
-    for r in range(n_orb):
-        for q in range(2):
-            occ[r, :, q * half : (q + 1) * half] = jnp.broadcast_to(
-                occupation[q, r : r + 1, :].astype(F32), (rows, half)
-            )
+    for q in range(2):
+        for r in range(2):
+            for c in range(0, half, LANES):
+                occ[(q * half + c) // LANES, pl.ds(r, n_orb, stride=2), :] = (
+                    occupation[q, :, c : c + LANES].astype(F32)
+                )
 
     def wait_mate(d, _):
         for h in range(n_grp):
@@ -363,29 +379,47 @@
     strings_three[n_strings : 2 * n_strings, :] = high
     strings_three[2 * n_strings :, :] = low
 
-    def mix_two(i, _):
-        d = 2 * i + 1
-        tos = [lax.rem(chip + d, n_chip), lax.rem(chip + d + 1, n_chip)]
-        y = jnp.dot(
-            jnp.concatenate([m_three[to] for to in tos], axis=0),
-            strings_three[...],
-            preferred_element_type=F32,
-        )
-        for q in range(2):
-            total = y[q * n_m : q * n_m + rows] * occ[0]
-            for r in range(1, n_orb):
-                total += y[q * n_m + r * rows : q * n_m + (r + 1) * rows] * occ[r]
-            staged[tos[q]] = total
-        back(d).start()
-
-        @pl.when(d + 1 < n_chip)
+    def reduce_rows(y):
+        sublane = lax.broadcasted_iota(jnp.int32, (rows, cut), 0)
+        factor = [
+            jnp.concatenate([occ[c, r : r + rows, :] for c in range(cut // LANES)], axis=1)
+            for r in range(0, n_r, rows)
+        ]
+        total = None
+        for p in range(rows // 2):
+            z = y[p * n_r : p * n_r + rows] * factor[0]
+            for r in range(rows, n_r, rows):
+                z += y[p * n_r + r : p * n_r + r + rows] * factor[r // rows]
+            z += pltpu.roll(z, 4, 0)
+            z += pltpu.roll(z, 2, 0)
+            total = z if total is None else jnp.where(sublane // 2 == p, z, total)
+        return total
+
+    def mix_four(i, _):
+        d = 4 * i + 1
+        tos = [lax.rem(chip + d + q, n_chip) for q in range(4)]
+        for q in (0, 2):
+            y = jnp.dot(
+                jnp.concatenate([m_three[to] for to in tos[q : q + 2]], axis=0),
+                strings_three[...],
+                preferred_element_type=F32,
+            )
+            staged[tos[q]] = reduce_rows(y[:n_m])
+            staged[tos[q + 1]] = reduce_rows(y[n_m:])
+        for q in range(3):
+            back(d + q).start()
+
+        @pl.when(d + 3 < n_chip)
         def _():
-            back(d + 1).start()
-
-        return 0
-
-    lax.fori_loop(0, n_chip // 2, mix_two, 0)
-
+            back(d + 3).start()
+
+        return 0
+
+    lax.fori_loop(0, n_chip // 4, mix_four, 0)
+    own = pltpu.make_async_copy(staged.at[chip], mixed.at[:, columns(chip)], out_sem.at[0])
+    own.start()
+
+    fetches[6].wait()
     place = jnp.where(
         lax.broadcasted_iota(jnp.int32, (n_blocks, p_size), 0)
         == jnp.broadcast_to(blocks[1:2, :], (n_blocks, p_size)),
@@ -422,24 +456,17 @@
                 c = partner[h, :, at]
                 for s in range(rows):
                     total += factors[h][s] * jnp.broadcast_to(c[s : s + 1, :], (rows, size))
-            out[:, at] = total
+            same_vmem[:, at] = total
         return 0
 
     lax.fori_loop(0, n_blocks // 4, couple, 0)
 
-    out[:, columns(chip)] += staged[chip]
-
-    def gather_up(d, _):
-        back(d).wait_recv()
-        who = lax.rem(chip - d + n_chip, n_chip)
-        out[:, columns(who)] += arrived[who]
-        return 0
-
-    lax.fori_loop(1, n_chip, gather_up, 0)
+    write = pltpu.make_async_copy(same_vmem, same, out_sem.at[1])
+    write.start()
 
     def drain(d, _):
         go(d).wait_send()
-        back(d).wait_send()
+        back(d).wait()
         return 0
 
     lax.fori_loop(1, n_chip, drain, 0)
@@ -455,6 +482,8 @@
     occ_copy.wait_send()
     for h in range(1, n_grp):
         across(h).wait_send()
+    own.wait()
+    write.wait()
 
 
 def fused(n_grp, n_wide, args):
@@ -464,7 +493,8 @@
     n_chip = n_wide // 2
     cut = width // n_chip
     n_orb, n_pair = coulomb.shape
-    n_m = n_orb * rows
+    n_r = -(-n_orb // 4) * 8
+    n_m = rows // 2 * n_r
     n_strings = n_grp * n_wide * rows
     table_width = -(-n_pair // LANES) * LANES
     p_size, size = beta.shape[:2]
@@ -477,21 +507,21 @@
         pltpu.VMEM((3 * n_strings, cut), BF16),
         pltpu.VMEM((n_grp, rows, width), F32),
         pltpu.VMEM((n_chip, rows, cut), F32),
-        pltpu.VMEM((n_chip, rows, cut), F32),
-        pltpu.VMEM((rows * p_size, size), F32),
-        pltpu.VMEM((rows * p_size, size), F32),
+        pltpu.VMEM((rows, width), F32),
+        pltpu.VMEM((width // size, rows, size), F32),
+        pltpu.SMEM(blocks.shape, blocks.dtype),
         pltpu.VMEM((rows * p_size, size), F32),
         pltpu.VMEM((width // size * rows, size), F32),
         pltpu.VMEM((LANES, LANES), jnp.int32),
         pltpu.VMEM((LANES, LANES), jnp.int32),
         pltpu.VMEM((LANES, LANES), jnp.int32),
         pltpu.VMEM((LANES, LANES), F32),
-        pltpu.VMEM((-(-n_orb // 8) * 8, table_width), F32),
-        pltpu.VMEM((n_orb, rows, cut), F32),
-        pltpu.VMEM((2 * n_m, rows * LANES), BF16),
-        pltpu.VMEM((rows * LANES, n_strings), BF16),
+        pltpu.VMEM((n_orb, table_width), F32),
+        pltpu.VMEM((table_width // LANES, n_r, LANES), F32),
+        pltpu.VMEM((cut // LANES, n_r, LANES), F32),
         pltpu.VMEM((n_chip, n_m, 3 * n_strings), BF16),
-        dma((len(operands),)),
+        dma((len(operands) + 1,)),
+        dma((2,)),
         dma((n_chip,)),
         dma((n_chip,)),
         dma((n_grp, n_chip)),
@@ -505,16 +535,17 @@
         dma((n_grp,)),
         dma((n_grp,)),
     ]
-    return pl.pallas_call(
+    same, mixed = pl.pallas_call(
         functools.partial(kernel, n_grp, n_wide),
-        out_shape=jax.ShapeDtypeStruct(coeff.shape, F32),
+        out_shape=[jax.ShapeDtypeStruct(coeff.shape, F32)] * 2,
         in_specs=[pl.BlockSpec(memory_space=pltpu.HBM)] * len(operands),
-        out_specs=pl.BlockSpec(memory_space=pltpu.VMEM),
+        out_specs=[pl.BlockSpec(memory_space=pltpu.HBM)] * 2,
         scratch_shapes=scratch,
         compiler_params=pltpu.CompilerParams(
             collective_id=0, has_side_effects=True, vmem_limit_bytes=64 * 2**20 - 2**16
         ),
     )(*operands)
+    return same + mixed
 
 
 def suits(n_grp, n_wide, args):
@@ -525,7 +556,7 @@
     return (
         n_grp > 1
         and n_wide > 2
-        and n_wide % 4 == 0
+        and n_wide % 8 == 0
         and rows == 8
         and width % (n_wide * LANES) == 0
         and beta.shape[1] == LANES

time: 26.8 us -> 26.3 us (0.981)
  other arithmetic: 0 us -> 1.72 us
  local copies, waits for them, and re-layouts: 1.62 us -> 0 us
  Pallas kernels: 25 us -> 24.4 us
    add x0 -> x1, other arithmetic: none -> 1.72 us  [fused(): return same + mixed]
    unnamed x1 -> x0, local copies, waits for them, and re-layouts: 1.62 us -> none
    pallas_call x1, Pallas kernels: 25 us -> 24.4 us  [fused(): pl.pallas_call(functools.partial(kernel, n_grp, n_wide), out_shape=[jax.S...]
where the time goes in v3:
time: 26.3 us; the launch traced here: 26.1 us
  Pallas kernels  24.4 us (93%)
  other arithmetic  1.72 us (7%)
    pallas_call x1, Pallas kernels, fused(): pl.pallas_call(functools.partial(kernel, n_grp, n_wide), out_shape=[jax.S...  24.4 us
    add x1, other arithmetic, fused(): return same + mixed  1.72 us

profile of v3, /device:TPU:0, one launch (start us, length us, event | category | flops | bytes accessed | tf_op | source)
XLA Modules:
  0.0 26.1 jit_solution(8210676015076627557)
XLA Ops:
  0.0 24.4 %shard_map.100 = (f32[8,6144]{1,0:T(8,128)}, f32[8,6144]{1,0:T(8,128)}) custom-call(f32[8,6144]{1,0:T(8,128)} %coeff_hbm.1, f32[96,128,128]{2,1,0:T(8,128)} %beta_hbm.1, s32[2,96]{1,0:T(2,128)} %blocks_hbm.1, f32[1,2,8,8]{3,2,1,0:T(8,128)} %alpha_hbm.1, s32[1,2]{1,0:T(1,128)} %mask_hbm.1, s32[90,128]{1,0:T(8,128)} %source_hbm.1, s32[90,128]{1,0:T(8,128)} %pair_hbm.1, ...), custom_call_target="tpu_custom_call" | custom-call | tf_op jit(solution)/shard_map/pallas_call | solution.py:538
  24.4 1.7 %add.3 = f32[8,6144]{1,0:T(8,128)} add(f32[8,6144]{1,0:T(8,128)} %get-tuple-element.7, f32[8,6144]{1,0:T(8,128)} %get-tuple-element.8) | non-fusion elementwise | flops 49152 | bytes 589824 | tf_op jit(solution)/shard_map/add | solution.py:548

commit v4 on v3

--- a/solution.py
+++ b/solution.py
@@ -202,11 +202,15 @@
             device_id_type=MESH,
         )
 
-    def start_go(d, _):
-        go(d).start()
-        return 0
-
-    lax.fori_loop(1, n_chip, start_go, 0)
+    def far_first(k):
+        half = (k + 1) // 2
+        return n_chip // 2 + half - 2 * half * lax.rem(k, 2)
+
+    def start_go(k, _):
+        go(far_first(k)).start()
+        return 0
+
+    lax.fori_loop(0, n_chip - 1, start_go, 0)
     occ_copy.start()
 
     padded[...] = jnp.zeros_like(padded)
@@ -319,44 +323,15 @@
         to_mate(d, 0).start()
 
     lax.fori_loop(0, n_chip // 2, build_and_pass, 0)
-    for h in range(1, n_grp):
-        across(h).start()
-
-    fetches[10].wait()
-    for t in range(n_blocks):
-        tiles[t] = coeff[:, t * size : (t + 1) * size]
-    fetches[9].wait()
-
-    def pick(k):
-        high, low = split_two(tiles[blocks_smem[0, k]])
-        return [
-            jnp.concatenate([high, high], axis=1),
-            jnp.concatenate([low, jnp.zeros_like(low)], axis=1),
-        ]
-
-    share = p_size // n_chip
-
-    def dense_and_pass(d, _):
-        results = []
-        for i in range(0, share, 2):
-            k = d * share + i
-            lhs = jnp.concatenate(pick(k) + pick(k + 1), axis=0).astype(BF16)
-            h0, l0 = split_narrow(dense[k])
-            h1, l1 = split_narrow(dense[k + 1])
-            rhs = jnp.concatenate(
-                [jnp.concatenate([h0, h1], axis=1), jnp.concatenate([l0, l1], axis=1)], axis=0
-            )
-            y = jnp.dot(lhs, rhs, preferred_element_type=F32)
-            results.append(y[0:rows, :size] + y[rows : 2 * rows, :size])
-            results.append(y[2 * rows : 3 * rows, size:] + y[3 * rows :, size:])
-        for i, result in enumerate(results):
-            applied[pl.ds(d * share + i, rows, stride=p_size), :] = result
+    def pass_relayed(d, _):
         for h in range(1, n_grp):
             relay(d, h).wait_recv()
             to_mate(d, h).start()
         return 0
 
-    lax.fori_loop(0, n_chip, dense_and_pass, 0)
+    lax.fori_loop(0, n_chip, pass_relayed, 0)
+    for h in range(1, n_grp):
+        across(h).start()
 
     fetches[4].wait()
     occ_copy.wait_recv()
@@ -395,29 +370,60 @@
             total = z if total is None else jnp.where(sublane // 2 == p, z, total)
         return total
 
-    def mix_four(i, _):
-        d = 4 * i + 1
-        tos = [lax.rem(chip + d + q, n_chip) for q in range(4)]
-        for q in (0, 2):
-            y = jnp.dot(
-                jnp.concatenate([m_three[to] for to in tos[q : q + 2]], axis=0),
-                strings_three[...],
-                preferred_element_type=F32,
-            )
-            staged[tos[q]] = reduce_rows(y[:n_m])
-            staged[tos[q + 1]] = reduce_rows(y[n_m:])
-        for q in range(3):
-            back(d + q).start()
-
-        @pl.when(d + 3 < n_chip)
+    def mix_two(i, _):
+        ds = [far_first(2 * i), far_first(2 * i + 1)]
+        tos = [lax.rem(chip + d, n_chip) for d in ds]
+        y = jnp.dot(
+            jnp.concatenate([m_three[to] for to in tos], axis=0),
+            strings_three[...],
+            preferred_element_type=F32,
+        )
+        for q in range(2):
+            staged[tos[q]] = reduce_rows(y[q * n_m : (q + 1) * n_m])
+        back(ds[0]).start()
+
+        @pl.when(i < n_chip // 2 - 1)
         def _():
-            back(d + 3).start()
-
-        return 0
-
-    lax.fori_loop(0, n_chip // 4, mix_four, 0)
+            back(ds[1]).start()
+
+        return 0
+
+    lax.fori_loop(0, n_chip // 2, mix_two, 0)
     own = pltpu.make_async_copy(staged.at[chip], mixed.at[:, columns(chip)], out_sem.at[0])
     own.start()
+
+    fetches[10].wait()
+    for t in range(n_blocks):
+        tiles[t] = coeff[:, t * size : (t + 1) * size]
+    fetches[9].wait()
+
+    def pick(k):
+        high, low = split_two(tiles[blocks_smem[0, k]])
+        return [
+            jnp.concatenate([high, high], axis=1),
+            jnp.concatenate([low, jnp.zeros_like(low)], axis=1),
+        ]
+
+    share = p_size // n_chip
+
+    def apply_dense(d, _):
+        results = []
+        for i in range(0, share, 2):
+            k = d * share + i
+            lhs = jnp.concatenate(pick(k) + pick(k + 1), axis=0).astype(BF16)
+            h0, l0 = split_narrow(dense[k])
+            h1, l1 = split_narrow(dense[k + 1])
+            rhs = jnp.concatenate(
+                [jnp.concatenate([h0, h1], axis=1), jnp.concatenate([l0, l1], axis=1)], axis=0
+            )
+            y = jnp.dot(lhs, rhs, preferred_element_type=F32)
+            results.append(y[0:rows, :size] + y[rows : 2 * rows, :size])
+            results.append(y[2 * rows : 3 * rows, size:] + y[3 * rows :, size:])
+        for i, result in enumerate(results):
+            applied[pl.ds(d * share + i, rows, stride=p_size), :] = result
+        return 0
+
+    lax.fori_loop(0, n_chip, apply_dense, 0)
 
     fetches[6].wait()
     place = jnp.where(

time: 26.3 us -> 26.8 us (1.019)
  Pallas kernels: 24.4 us -> 24.9 us
    pallas_call x1, Pallas kernels: 24.4 us -> 24.9 us  [fused(): pl.pallas_call(functools.partial(kernel, n_grp, n_wide), out_shape=[jax.S...]
where the time goes in v4:
time: 26.8 us; the launch traced here: 26.6 us
  Pallas kernels  24.9 us (93%)
  other arithmetic  1.72 us (6%)
    pallas_call x1, Pallas kernels, fused(): pl.pallas_call(functools.partial(kernel, n_grp, n_wide), out_shape=[jax.S...  24.9 us
    add x1, other arithmetic, fused(): return same + mixed  1.72 us

profile of v4, /device:TPU:0, one launch (start us, length us, event | category | flops | bytes accessed | tf_op | source)
XLA Modules:
  0.0 26.6 jit_solution(17635423799688407142)
XLA Ops:
  0.0 24.9 %shard_map.100 = (f32[8,6144]{1,0:T(8,128)}, f32[8,6144]{1,0:T(8,128)}) custom-call(f32[8,6144]{1,0:T(8,128)} %coeff_hbm.1, f32[96,128,128]{2,1,0:T(8,128)} %beta_hbm.1, s32[2,96]{1,0:T(2,128)} %blocks_hbm.1, f32[1,2,8,8]{3,2,1,0:T(8,128)} %alpha_hbm.1, s32[1,2]{1,0:T(1,128)} %mask_hbm.1, s32[90,128]{1,0:T(8,128)} %source_hbm.1, s32[90,128]{1,0:T(8,128)} %pair_hbm.1, ...), custom_call_target="tpu_custom_call" | custom-call | tf_op jit(solution)/shard_map/pallas_call | solution.py:544
  24.9 1.7 %add.3 = f32[8,6144]{1,0:T(8,128)} add(f32[8,6144]{1,0:T(8,128)} %get-tuple-element.7, f32[8,6144]{1,0:T(8,128)} %get-tuple-element.8) | non-fusion elementwise | flops 49152 | bytes 589824 | tf_op jit(solution)/shard_map/add | solution.py:554

commit v5 on v4

--- a/solution.py
+++ b/solution.py
@@ -92,7 +92,8 @@
     exc = source.shape[0]
     n_orb, n_pair = coulomb.shape
     chunks = table.shape[0]
-    n_strings = n_grp * n_wide * rows
+    n_own = n_wide * rows
+    n_strings = n_grp * n_own
     n_r = -(-n_orb // 4) * 8
     n_m = rows // 2 * n_r
     p_size, size = dense.shape[:2]
@@ -138,14 +139,13 @@
         return pl.ds(pl.multiple_of(j * cut, LANES), cut)
 
     def slot(d, h):
-        group = lax.rem(g - h + n_grp, n_grp)
-        return group * n_wide + 2 * lax.rem(chip - d + n_chip, n_chip) + core
+        return h * n_wide + 2 * lax.rem(chip - d + n_chip, n_chip) + core
 
     def go(d):
         to = lax.rem(chip + d, n_chip)
         return pltpu.make_async_remote_copy(
             src_ref=coeff_hbm.at[:, columns(to)],
-            dst_ref=strings.at[g * n_wide + w],
+            dst_ref=strings.at[w],
             send_sem=go_send.at[d],
             recv_sem=go_recv.at[d],
             device_id=(g, 2 * to + core),
@@ -155,7 +155,7 @@
     def relay(d, h):
         return pltpu.make_async_remote_copy(
             src_ref=strings.at[slot(d, 0)],
-            dst_ref=strings.at[slot(d, 0)],
+            dst_ref=strings.at[slot(d, h)],
             send_sem=relay_send.at[h, d],
             recv_sem=relay_recv.at[h, d],
             device_id=(lax.rem(g + h, n_grp), w),
@@ -224,7 +224,9 @@
     sign_t[...] = padded[...].T.astype(F32)
     source_pad[...] = jnp.zeros_like(source_pad)
     fetches[2].wait()
-    source_pad[0:exc, :] = source[...]
+    group = source[...] // n_own
+    before = lax.rem(g + n_grp - group, n_grp)
+    source_pad[0:exc, :] = before * n_own + source[...] - group * n_own
     fetches[3].wait()
     coulomb_pad[...] = jnp.zeros_like(coulomb_pad)
     coulomb_pad[:, 0:n_pair] = coulomb[...]
@@ -233,7 +235,7 @@
             line = coulomb_pad[:, c * LANES : (c + 1) * LANES]
             table[c, pl.ds(q, n_orb, stride=2), :] = line
     fetches[5].wait()
-    strings[g * n_wide + w] = coeff[:, columns(chip)]
+    strings[w] = coeff[:, columns(chip)]
     partner[g] = coeff[...]
     for h in range(1, n_grp):
         relay(0, h).start()
@@ -305,9 +307,12 @@
     def build_and_pass(i, _):
         d = 2 * i
         for to, (high, low) in [(q, build(q)) for q in (d, d + 1)]:
-            m_three[to, :, 0:n_strings] = high
-            m_three[to, :, n_strings : 2 * n_strings] = low
-            m_three[to, :, 2 * n_strings :] = high
+            for h in range(n_grp):
+                own = slice(h * n_own, (h + 1) * n_own)
+                at = 3 * h * n_own
+                m_three[to, :, at : at + n_own] = high[:, own]
+                m_three[to, :, at + n_own : at + 2 * n_own] = low[:, own]
+                m_three[to, :, at + 2 * n_own : at + 3 * n_own] = high[:, own]
 
         @pl.when(i > 0)
         def _():
@@ -323,16 +328,6 @@
         to_mate(d, 0).start()
 
     lax.fori_loop(0, n_chip // 2, build_and_pass, 0)
-    def pass_relayed(d, _):
-        for h in range(1, n_grp):
-            relay(d, h).wait_recv()
-            to_mate(d, h).start()
-        return 0
-
-    lax.fori_loop(0, n_chip, pass_relayed, 0)
-    for h in range(1, n_grp):
-        across(h).start()
-
     fetches[4].wait()
     occ_copy.wait_recv()
     half = occupation.shape[2]
@@ -343,16 +338,21 @@
                     occupation[q, :, c : c + LANES].astype(F32)
                 )
 
-    def wait_mate(d, _):
-        for h in range(n_grp):
+    def narrow(h):
+        own = strings[h * n_wide : (h + 1) * n_wide].reshape(n_own, cut)
+        high, low = split_narrow(own)
+        at = 3 * h * n_own
+        strings_three[at : at + n_own, :] = high
+        strings_three[at + n_own : at + 2 * n_own, :] = high
+        strings_three[at + 2 * n_own : at + 3 * n_own, :] = low
+
+    def wait_mate(h):
+        def wait(d, _):
             to_mate(d, h).wait_recv()
-        return 0
-
-    lax.fori_loop(0, n_chip, wait_mate, 0)
-    high, low = split_narrow(strings[...].reshape(n_strings, cut))
-    strings_three[0:n_strings, :] = high
-    strings_three[n_strings : 2 * n_strings, :] = high
-    strings_three[2 * n_strings :, :] = low
+            return 0
+
+        lax.fori_loop(0, n_chip, wait, 0)
+        narrow(h)
 
     def reduce_rows(y):
         sublane = lax.broadcasted_iota(jnp.int32, (rows, cut), 0)
@@ -370,16 +370,30 @@
             total = z if total is None else jnp.where(sublane // 2 == p, z, total)
         return total
 
-    def mix_two(i, _):
+    def mix(i, columns_of):
         ds = [far_first(2 * i), far_first(2 * i + 1)]
         tos = [lax.rem(chip + d, n_chip) for d in ds]
         y = jnp.dot(
-            jnp.concatenate([m_three[to] for to in tos], axis=0),
-            strings_three[...],
+            jnp.concatenate([m_three[to, :, columns_of] for to in tos], axis=0),
+            strings_three[columns_of, :],
             preferred_element_type=F32,
         )
-        for q in range(2):
-            staged[tos[q]] = reduce_rows(y[q * n_m : (q + 1) * n_m])
+        return ds, tos, [reduce_rows(y[q * n_m : (q + 1) * n_m]) for q in range(2)]
+
+    def mix_own(i, _):
+        _, tos, sums = mix(i, slice(0, 3 * n_own))
+        for to, total in zip(tos, sums):
+            staged[to] = total
+        for d in (2 * i, 2 * i + 1):
+            for h in range(1, n_grp):
+                relay(d, h).wait_recv()
+                to_mate(d, h).start()
+        return 0
+
+    def mix_rest(i, _):
+        ds, tos, sums = mix(i, slice(3 * n_own, 3 * n_strings))
+        for to, total in zip(tos, sums):
+            staged[to] += total
         back(ds[0]).start()
 
         @pl.when(i < n_chip // 2 - 1)
@@ -388,9 +402,10 @@
 
         return 0
 
-    lax.fori_loop(0, n_chip // 2, mix_two, 0)
-    own = pltpu.make_async_copy(staged.at[chip], mixed.at[:, columns(chip)], out_sem.at[0])
-    own.start()
+    wait_mate(0)
+    lax.fori_loop(0, n_chip // 2, mix_own, 0)
+    for h in range(1, n_grp):
+        across(h).start()
 
     fetches[10].wait()
     for t in range(n_blocks):
@@ -423,7 +438,14 @@
             applied[pl.ds(d * share + i, rows, stride=p_size), :] = result
         return 0
 
-    lax.fori_loop(0, n_chip, apply_dense, 0)
+    lax.fori_loop(0, n_chip // 2, apply_dense, 0)
+    for h in range(1, n_grp):
+        wait_mate(h)
+    lax.fori_loop(0, n_chip // 2, mix_rest, 0)
+    own = pltpu.make_async_copy(staged.at[chip], mixed.at[:, columns(chip)], out_sem.at[0])
+    own.start()
+
+    lax.fori_loop(n_chip // 2, n_chip, apply_dense, 0)
 
     fetches[6].wait()
     place = jnp.where(

time: 26.8 us -> 26.9 us (level)
  no operation moved by 1% of the time
where the time goes in v5:
time: 26.9 us; the launch traced here: 26.8 us
  Pallas kernels  25.1 us (93%)
  other arithmetic  1.72 us (6%)
    pallas_call x1, Pallas kernels, fused(): pl.pallas_call(functools.partial(kernel, n_grp, n_wide), out_shape=[jax.S...  25.1 us
    add x1, other arithmetic, fused(): return same + mixed  1.72 us

profile of v5, /device:TPU:0, one launch (start us, length us, event | category | flops | bytes accessed | tf_op | source)
XLA Modules:
  0.0 26.8 jit_solution(9533466265767799062)
XLA Ops:
  0.0 25.1 %shard_map.100 = (f32[8,6144]{1,0:T(8,128)}, f32[8,6144]{1,0:T(8,128)}) custom-call(f32[8,6144]{1,0:T(8,128)} %coeff_hbm.1, f32[96,128,128]{2,1,0:T(8,128)} %beta_hbm.1, s32[2,96]{1,0:T(2,128)} %blocks_hbm.1, f32[1,2,8,8]{3,2,1,0:T(8,128)} %alpha_hbm.1, s32[1,2]{1,0:T(1,128)} %mask_hbm.1, s32[90,128]{1,0:T(8,128)} %source_hbm.1, s32[90,128]{1,0:T(8,128)} %pair_hbm.1, ...), custom_call_target="tpu_custom_call" | custom-call | tf_op jit(solution)/shard_map/pallas_call | solution.py:566
  25.1 1.7 %add.3 = f32[8,6144]{1,0:T(8,128)} add(f32[8,6144]{1,0:T(8,128)} %get-tuple-element.7, f32[8,6144]{1,0:T(8,128)} %get-tuple-element.8) | non-fusion elementwise | flops 49152 | bytes 589824 | tf_op jit(solution)/shard_map/add | solution.py:576

commit v6 on v3

--- a/solution.py
+++ b/solution.py
@@ -59,7 +59,7 @@
     applied,
     placed,
     padded,
-    source_pad,
+    source_t,
     pair_t,
     sign_t,
     coulomb_pad,
@@ -218,9 +218,9 @@
     fetches[1].wait()
     padded[0:exc, :] = 1 - 2 * parity[...]
     sign_t[...] = padded[...].T.astype(F32)
-    source_pad[...] = jnp.zeros_like(source_pad)
     fetches[2].wait()
-    source_pad[0:exc, :] = source[...]
+    padded[0:exc, :] = source[...]
+    source_t[...] = padded[...].T
     fetches[3].wait()
     coulomb_pad[...] = jnp.zeros_like(coulomb_pad)
     coulomb_pad[:, 0:n_pair] = coulomb[...]
@@ -240,7 +240,8 @@
         at = pl.ds(pl.multiple_of(block * rows, rows), rows)
         sublane = lax.broadcasted_iota(jnp.int32, (rows, LANES), 0)
         odd = sublane - sublane // 2 * 2 == 1
-        string = lax.broadcasted_iota(jnp.int32, (16, n_strings), 1)
+        string = lax.broadcasted_iota(jnp.int32, (n_strings, LANES), 0)
+        sources = source_t[at, :]
         all_pairs = pair_t[at, :]
         all_signs = sign_t[at, :]
 
@@ -253,25 +254,12 @@
 
         found = []
         for a in range(0, rows, 2):
-            hits = []
-            for b in (a, a + 1):
-                column = jnp.full((rows, LANES), block * rows + b, jnp.int32)
-                for e in range(0, LANES, 16):
-                    if e >= exc:
-                        hits.append(jnp.zeros((16, n_strings), BF16))
-                        continue
-                    pieces = [
-                        jnp.take_along_axis(
-                            source_pad[e + f : e + f + rows, :],
-                            column,
-                            axis=1,
-                            mode="promise_in_bounds",
-                        )
-                        for f in (0, 8)
-                    ]
-                    both = jnp.concatenate(pieces, axis=0)
-                    full = jnp.concatenate([both] * (n_strings // LANES), axis=1)
-                    hits.append(jnp.where(full == string, 1.0, 0.0).astype(BF16))
+            hits = [
+                jnp.where(
+                    string == jnp.broadcast_to(sources[b : b + 1, :], (n_strings, LANES)), 1.0, 0.0
+                ).astype(BF16)
+                for b in (a, a + 1)
+            ]
             pairs = of_two(all_pairs, a)
             signs = of_two(all_signs, a)
             which = pairs // LANES
@@ -294,7 +282,12 @@
                         )
                     )
             left = jnp.concatenate(parts[0] + parts[1], axis=0).astype(BF16)
-            m = jnp.dot(left, jnp.concatenate(hits, axis=0), preferred_element_type=F32)
+            m = lax.dot_general(
+                left,
+                jnp.concatenate(hits, axis=1),
+                (((1,), (1,)), ((), ())),
+                preferred_element_type=F32,
+            )
             found.append(m[:n_r] + m[n_r:])
         return split_narrow(jnp.concatenate(found, axis=0))
 

time: 26.3 us -> 26 us (0.989)
  Pallas kernels: 24.4 us -> 24.1 us
    pallas_call x1, Pallas kernels: 24.4 us -> 24.1 us  [fused(): pl.pallas_call(functools.partial(kernel, n_grp, n_wide), out_shape=[jax.S...]
where the time goes in v6:
time: 26 us; the launch traced here: 25.9 us
  Pallas kernels  24.1 us (93%)
  other arithmetic  1.72 us (7%)
    pallas_call x1, Pallas kernels, fused(): pl.pallas_call(functools.partial(kernel, n_grp, n_wide), out_shape=[jax.S...  24.1 us
    add x1, other arithmetic, fused(): return same + mixed  1.72 us

profile of v6, /device:TPU:0, one launch (start us, length us, event | category | flops | bytes accessed | tf_op | source)
XLA Modules:
  0.0 25.9 jit_solution(10857273460145538089)
XLA Ops:
  0.0 24.1 %shard_map.100 = (f32[8,6144]{1,0:T(8,128)}, f32[8,6144]{1,0:T(8,128)}) custom-call(f32[8,6144]{1,0:T(8,128)} %coeff_hbm.1, f32[96,128,128]{2,1,0:T(8,128)} %beta_hbm.1, s32[2,96]{1,0:T(2,128)} %blocks_hbm.1, f32[1,2,8,8]{3,2,1,0:T(8,128)} %alpha_hbm.1, s32[1,2]{1,0:T(1,128)} %mask_hbm.1, s32[90,128]{1,0:T(8,128)} %source_hbm.1, s32[90,128]{1,0:T(8,128)} %pair_hbm.1, ...), custom_call_target="tpu_custom_call" | custom-call | tf_op jit(solution)/shard_map/pallas_call | solution.py:531
  24.1 1.7 %add.3 = f32[8,6144]{1,0:T(8,128)} add(f32[8,6144]{1,0:T(8,128)} %get-tuple-element.7, f32[8,6144]{1,0:T(8,128)} %get-tuple-element.8) | non-fusion elementwise | flops 49152 | bytes 589824 | tf_op jit(solution)/shard_map/add | solution.py:541

commit v7 on v6

--- a/solution.py
+++ b/solution.py
@@ -202,11 +202,15 @@
             device_id_type=MESH,
         )
 
-    def start_go(d, _):
-        go(d).start()
-        return 0
-
-    lax.fori_loop(1, n_chip, start_go, 0)
+    def far_first(k):
+        half = (k + 1) // 2
+        return n_chip // 2 + half - 2 * half * lax.rem(k, 2)
+
+    def start_go(k, _):
+        go(far_first(k)).start()
+        return 0
+
+    lax.fori_loop(0, n_chip - 1, start_go, 0)
     occ_copy.start()
 
     padded[...] = jnp.zeros_like(padded)
@@ -312,8 +316,6 @@
         to_mate(d, 0).start()
 
     lax.fori_loop(0, n_chip // 2, build_and_pass, 0)
-    for h in range(1, n_grp):
-        across(h).start()
 
     fetches[10].wait()
     for t in range(n_blocks):
@@ -350,6 +352,8 @@
         return 0
 
     lax.fori_loop(0, n_chip, dense_and_pass, 0)
+    for h in range(1, n_grp):
+        across(h).start()
 
     fetches[4].wait()
     occ_copy.wait_recv()
@@ -388,27 +392,25 @@
             total = z if total is None else jnp.where(sublane // 2 == p, z, total)
         return total
 
-    def mix_four(i, _):
-        d = 4 * i + 1
-        tos = [lax.rem(chip + d + q, n_chip) for q in range(4)]
-        for q in (0, 2):
-            y = jnp.dot(
-                jnp.concatenate([m_three[to] for to in tos[q : q + 2]], axis=0),
-                strings_three[...],
-                preferred_element_type=F32,
-            )
-            staged[tos[q]] = reduce_rows(y[:n_m])
-            staged[tos[q + 1]] = reduce_rows(y[n_m:])
-        for q in range(3):
-            back(d + q).start()
-
-        @pl.when(d + 3 < n_chip)
+    def mix_two(i, _):
+        ds = [far_first(2 * i), far_first(2 * i + 1)]
+        tos = [lax.rem(chip + d, n_chip) for d in ds]
+        y = jnp.dot(
+            jnp.concatenate([m_three[to] for to in tos], axis=0),
+            strings_three[...],
+            preferred_element_type=F32,
+        )
+        for q in range(2):
+            staged[tos[q]] = reduce_rows(y[q * n_m : (q + 1) * n_m])
+        back(ds[0]).start()
+
+        @pl.when(i < n_chip // 2 - 1)
         def _():
-            back(d + 3).start()
-
-        return 0
-
-    lax.fori_loop(0, n_chip // 4, mix_four, 0)
+            back(ds[1]).start()
+
+        return 0
+
+    lax.fori_loop(0, n_chip // 2, mix_two, 0)
     own = pltpu.make_async_copy(staged.at[chip], mixed.at[:, columns(chip)], out_sem.at[0])
     own.start()
 
@@ -446,9 +448,8 @@
             at = pl.ds(pl.multiple_of(t * size, size), size)
             total = placed[pl.ds(pl.multiple_of(t * rows, rows), rows), :]
             for h in range(n_grp):
-                c = partner[h, :, at]
                 for s in range(rows):
-                    total += factors[h][s] * jnp.broadcast_to(c[s : s + 1, :], (rows, size))
+                    total += factors[h][s] * jnp.broadcast_to(partner[h, s : s + 1, at], (rows, size))
             same_vmem[:, at] = total
         return 0
 

time: 26 us -> 26.6 us (1.023)
  Pallas kernels: 24.1 us -> 24.7 us
    pallas_call x1, Pallas kernels: 24.1 us -> 24.7 us  [fused(): pl.pallas_call(functools.partial(kernel, n_grp, n_wide), out_shape=[jax.S...]
where the time goes in v7:
time: 26.6 us; the launch traced here: 26.4 us
  Pallas kernels  24.7 us (93%)
  other arithmetic  1.72 us (6%)
    pallas_call x1, Pallas kernels, fused(): pl.pallas_call(functools.partial(kernel, n_grp, n_wide), out_shape=[jax.S...  24.7 us
    add x1, other arithmetic, fused(): return same + mixed  1.72 us

profile of v7, /device:TPU:0, one launch (start us, length us, event | category | flops | bytes accessed | tf_op | source)
XLA Modules:
  0.0 26.4 jit_solution(9782614717395560329)
XLA Ops:
  0.0 24.7 %shard_map.100 = (f32[8,6144]{1,0:T(8,128)}, f32[8,6144]{1,0:T(8,128)}) custom-call(f32[8,6144]{1,0:T(8,128)} %coeff_hbm.1, f32[96,128,128]{2,1,0:T(8,128)} %beta_hbm.1, s32[2,96]{1,0:T(2,128)} %blocks_hbm.1, f32[1,2,8,8]{3,2,1,0:T(8,128)} %alpha_hbm.1, s32[1,2]{1,0:T(1,128)} %mask_hbm.1, s32[90,128]{1,0:T(8,128)} %source_hbm.1, s32[90,128]{1,0:T(8,128)} %pair_hbm.1, ...), custom_call_target="tpu_custom_call" | custom-call | tf_op jit(solution)/shard_map/pallas_call | solution.py:532
  24.7 1.7 %add.3 = f32[8,6144]{1,0:T(8,128)} add(f32[8,6144]{1,0:T(8,128)} %get-tuple-element.7, f32[8,6144]{1,0:T(8,128)} %get-tuple-element.8) | non-fusion elementwise | flops 49152 | bytes 589824 | tf_op jit(solution)/shard_map/add | solution.py:542
